TPU v7x, 32 devices: a whole 2x2x4 slice. The times are simulated.
32 devices in a mesh: ep: 16 (over z, y, x), rep: 2 (over core).
Axes of the slice: x: 2, y: 2, z: 4, core: 2. Of those that a mesh axis runs over, the one named last changes fastest.
Arguments:
- dy: bfloat16 [512, 2048], P('ep'), may hold values from -6 to 6
- probs: float32 [512, 8], P('ep'), may hold values from 0.02 to 0.5
- expert_ids: int32 [512, 8], P('ep'), may hold values from 0 to 15, as said below
- copy_choice: int32 [512, 8], P('ep'), may hold values from 0 to 1, as said below
- saved_inputs: bfloat16 [16, 2, 16, 16, 2048], P('ep', 'rep'), may hold values from -24 to 24
- saved_gate: bfloat16 [16, 2, 16, 16, 768], P('ep', 'rep'), may hold values from -4 to 4
- saved_up: bfloat16 [16, 2, 16, 16, 768], P('ep', 'rep'), may hold values from -12 to 12
- down_weight: bfloat16 [16, 768, 2048], P('ep', None, 'rep'), may hold values from -4 to 4
- gate_weight: bfloat16 [16, 2048, 768], P('ep', 'rep'), may hold values from -4 to 4
- up_weight: bfloat16 [16, 2048, 768], P('ep', 'rep'), may hold values from -4 to 4
- new_owner: int32 [16], replicated, may hold values from 0 to 15, each once
Outputs:
- new_gate: bfloat16 [16, 2048, 768], P('ep', 'rep')
- new_up: bfloat16 [16, 2048, 768], P('ep', 'rep')
Inputs may be any that keep to these rules, and one draw needn't show every extreme that they name: `expert_ids`: each row names 8 different experts; the rows of one index of ep name each expert at most 2 * 16 times. `copy_choice`: of the pairs of the rows of one index of ep that name one expert, at most 16 take each copy; some take exactly 16 in every draw. `new_owner`: each expert has exactly one owner.
All inputs are finite; a program needn't handle non-finite values.
Results may differ from a plain program's by a relative error of at most 0.0056.
Values may be sent and summed in bfloat16 or wider, within the bound.
No kernel may reach another device: no remote copies, remote signals or barrier semaphores. Data moves between devices by JAX's collectives and lax.ppermute only.
A program may use at most 64 MiB of HBM per device.

v0:
```python
import math

import jax
import jax.numpy as jnp
from jax import lax
from jax.sharding import PartitionSpec as P

ITERS = 2


quintic_first = 3.4445
quintic_second = -4.775
quintic_third = 2.0315
step_scale = 2.0
epsilon = 1e-07


def from_partner(block, axis, stride):
    count = lax.axis_size(axis)
    route = []
    for low in range(count):
        high = low | 1 << stride
        if high != low and high < count:
            route += [(low, high), (high, low)]
    return lax.ppermute(block, axis, route)


def contract_rows(left, right):
    return lax.dot_general(
        left, right, (((0,), (0,)), ((), ())), preferred_element_type=jnp.float32
    )


def orthogonalize(gradient):
    total = jnp.sqrt(jnp.sum(gradient * gradient))
    iterate = lax.optimization_barrier((gradient / (total + epsilon)).astype(jnp.bfloat16))
    for repeat in range(ITERS):
        gram = lax.optimization_barrier(contract_rows(iterate, iterate).astype(jnp.bfloat16))
        square = jnp.dot(gram, gram, preferred_element_type=jnp.float32)
        poly = (quintic_second * gram.astype(jnp.float32) + quintic_third * square).astype(
            jnp.bfloat16
        )
        mixed = quintic_first * iterate.astype(jnp.float32) + jnp.dot(
            iterate, poly, preferred_element_type=jnp.float32
        )
        iterate = lax.optimization_barrier(mixed.astype(jnp.bfloat16))
    return iterate


def shards(
    dy,
    probs,
    expert_ids,
    copy_choice,
    saved_inputs,
    saved_gate,
    saved_up,
    down_weight,
    gate_weight,
    up_weight,
    new_owner,
):
    copy_index = lax.axis_index("rep")
    copy_count = lax.axis_size("rep")
    experts = lax.axis_size("ep")
    capacity = saved_inputs.shape[3]
    width = dy.shape[1]
    inner = saved_gate.shape[4]
    pair_count = expert_ids.shape[0] * expert_ids.shape[1]
    flat_ids = expert_ids.reshape(pair_count)
    flat_copy = copy_choice.reshape(pair_count)
    keyed = flat_ids * copy_count + flat_copy
    matches = (keyed[:, None] == jnp.arange(experts * copy_count, dtype=jnp.int32)[None, :]).astype(
        jnp.int32
    )
    position = jnp.sum(jnp.cumsum(matches, axis=0) * matches, axis=1) - 1
    target = jnp.where(flat_copy == copy_index, flat_ids * capacity + position, experts * capacity)
    scaled = (
        (probs[:, :, None] * dy.astype(jnp.float32)[:, None, :])
        .astype(jnp.bfloat16)
        .reshape(pair_count, width)
    )
    outgoing = (
        jnp.zeros((experts * capacity, width), jnp.bfloat16).at[target].set(scaled, mode="drop")
    )
    incoming = lax.all_to_all(
        outgoing.reshape(experts, capacity, width), "ep", split_axis=0, concat_axis=0, tiled=True
    )
    routed = incoming.reshape(experts * capacity, width)
    hidden_grad = lax.dot_general(
        routed,
        lax.all_gather(down_weight[0], "rep", axis=1, tiled=True),
        (((1,), (1,)), ((), ())),
        preferred_element_type=jnp.float32,
    ) / math.sqrt(inner)
    gate_value = saved_gate.reshape(-1, inner).astype(jnp.float32)
    up_value = saved_up.reshape(-1, inner).astype(jnp.float32)
    sigmoid = jax.nn.sigmoid(gate_value)
    gate_rows = (hidden_grad * up_value * sigmoid * (1.0 + gate_value * (1.0 - sigmoid))).astype(
        jnp.bfloat16
    )
    up_rows = (hidden_grad * gate_value * sigmoid).astype(jnp.bfloat16)
    inputs = saved_inputs.reshape(-1, width)
    both_rows = jnp.stack([gate_rows, up_rows])
    own_rows = lax.dynamic_index_in_dim(both_rows, copy_index, 0, keepdims=False)
    partner_rows = lax.dynamic_index_in_dim(both_rows, 1 - copy_index, 0, keepdims=False)
    other_inputs, other_rows = from_partner((inputs, partner_rows), "rep", 0)
    gradient = contract_rows(inputs, own_rows) + contract_rows(other_inputs, other_rows)
    ortho = orthogonalize(gradient)
    factor = step_scale * math.sqrt(width)
    halfway = width // 2
    inverse = (
        jnp.zeros((experts,), jnp.int32).at[new_owner].set(jnp.arange(experts, dtype=jnp.int32))
    )
    own_halves = jnp.stack([gate_weight[0], up_weight[0]])
    halves = lax.all_to_all(
        ortho.reshape(2, halfway, inner), "rep", split_axis=0, concat_axis=0, tiled=True
    )
    updated = (own_halves.astype(jnp.float32) - factor * halves.astype(jnp.float32)).astype(
        jnp.bfloat16
    )
    spread_out = lax.all_to_all(
        updated.reshape(2, experts, -1), "ep", split_axis=1, concat_axis=1, tiled=True
    )
    arranged = jnp.take(spread_out, inverse, axis=1)
    collected = lax.all_to_all(arranged, "ep", split_axis=1, concat_axis=1, tiled=True)
    result = collected.reshape(2, halfway, inner)
    return (result[0:1], result[1:2])


def solution(mesh):
    in_specs = (
        P("ep", None),
        P("ep", None),
        P("ep", None),
        P("ep", None),
        P("ep", "rep", None, None, None),
        P("ep", "rep", None, None, None),
        P("ep", "rep", None, None, None),
        P("ep", None, "rep"),
        P("ep", "rep", None),
        P("ep", "rep", None),
        P(),
    )
    out_specs = (P("ep", "rep", None), P("ep", "rep", None))
    return jax.shard_map(shards, mesh=mesh, in_specs=in_specs, out_specs=out_specs, check_vma=False)
```

profile of v0, /device:TPU:0, one launch (start us, length us, event | category | flops | bytes accessed | tf_op | source)
XLA Modules:
  0.0 301.6 jit_solution(178762272767726947)
XLA Ops:
  7.2 0.0 all-gather.3.cloned.1.call-start
  7.2 0.7 all-gather.3.cloned.1.call-update
  7.9 0.7 multiply_add_fusion
  8.6 0.1 copy.27
  8.7 0.1 add.88
  8.8 0.1 add.87
  8.9 0.6 reduce-window.6
  9.5 0.2 slice_reduce_fusion.2
  9.7 0.7 broadcast_compare_fusion
  10.4 0.1 copy.25
  10.5 0.1 eq.39
  10.6 0.1 copy.26
  10.7 0.1 mul.98
  10.8 0.9 convert_element_type.77
  11.7 0.8 copy.30
  12.5 0.1 mul.102
  12.6 0.1 fusion.29
  12.7 3.2 %scatter_custom_fusion.1 = bf16[256,2048]{1,0:T(8,128)(2,1)} fusion(s32[256]{0:T(256)S(1)} %bitcast.74, f32[32,2048]{1,0:T(8,128)S(1)} %convert_element_type.77, f32[256]{0:T(256)S(1)} %mul.102, bf16[]{:T(256)} %constant.17.clone.1), kind=kCustom, calls=%fused_computation.26 | custom fusion | flops 1048576 | bytes 1311746 | tf_op jit(solution)/shard_map/scatter | solution.py:84
  15.9 8.5 %all-to-all-start = ((bf16[16,16,2048]{2,1,0:T(8,128)(2,1)}), bf16[16,16,2048]{2,1,0:T(8,128)(2,1)S(1)}, u32[]{:S(2)}, u32[]{:S(2)}) async-start(bf16[16,16,2048]{2,1,0:T(8,128)(2,1)} %bitcast.4), calls=%async_computation | async-start | bytes 2097152 | tf_op jit(solution)/shard_map/all_to_all | solution.py:86
  24.4 0.1 collective-permute-start.1
  24.5 24.2 %all-to-all-done = bf16[16,16,2048]{2,1,0:T(8,128)(2,1)S(1)} async-done(((bf16[16,16,2048]{2,1,0:T(8,128)(2,1)}), bf16[16,16,2048]{2,1,0:T(8,128)(2,1)S(1)}, u32[]{:S(2)}, u32[]{:S(2)}) %all-to-all-start) | async-done | bytes 1048608 | tf_op jit(solution)/shard_map/all_to_all | solution.py:86
  48.7 3.2 %fusion.19 = (bf16[256,768]{1,0:T(8,128)(2,1)S(1)}, bf16[256,768]{1,0:T(8,128)(2,1)S(1)}) fusion(bf16[1,1,16,16,768]{4,3,2,1,0:T(8,128)(2,1)S(1)} %copy-done.3, bf16[1,1,16,16,768]{4,3,2,1,0:T(8,128)(2,1)} %param.17, bf16[256,2048]{1,0:T(8,128)(2,1)S(1)} %bitcast.72, bf16[1,768,2048]{2,1,0:T(8,128)(2,1)} %all-gather.3.cloned.1.call-done), kind=kOutput, calls=%fused_computation.40 | convolution fusion | flops 808452096 | bytes 5767168 | tf_op jit(solution)/shard_map/dot_general | solution.py:90
  51.9 0.2 fusion.23
  52.0 0.1 collective-permute-start
  52.1 1.1 fusion.26
  53.2 0.6 collective-permute-done
  53.8 4.4 %multiply_reduce_fusion = (f32[]{:T(128)}, f32[768,2048]{1,0:T(8,128)}) fusion(f32[768,2048]{1,0:T(8,128)S(1)} %fusion.26, bf16[256,768]{1,0:T(8,128)(2,1)S(1)} %collective-permute-done, bf16[256,2048]{1,0:T(8,128)(2,1)S(1)} %collective-permute-done.1), kind=kOutput, calls=%fused_computation.7 | convolution fusion | flops 810024960 | bytes 14024708 | tf_op jit(solution)/shard_map/dot_general | solution.py:29
  58.9 3.6 %fusion.3 = bf16[2048,768]{0,1:T(8,128)(2,1)S(1)} fusion(f32[768,2048]{1,0:T(8,128)} %get-tuple-element.9, f32[]{:T(128)S(6)} %add.96), kind=kLoop, calls=%fused_computation.15 | loop fusion | flops 3145728 | bytes 9437188 | tf_op jit(solution)/shard_map/convert_element_type | solution.py:36
  62.5 3.6 %convolution_convert_fusion.1 = bf16[768,768]{1,0:T(8,128)(2,1)} fusion(bf16[2048,768]{0,1:T(8,128)(2,1)S(1)} %fusion.3), kind=kOutput, calls=%fused_computation.21 | convolution fusion | flops 2416508928 | bytes 4325376 | tf_op jit(solution)/shard_map/dot_general | solution.py:29
  66.2 8.5 %add_convert_fusion.1 = bf16[2048,768]{0,1:T(8,128)(2,1)} fusion(bf16[2048,768]{0,1:T(8,128)(2,1)S(1)} %fusion.3, bf16[768,768]{1,0:T(8,128)(2,1)} %convolution_convert_fusion.1), kind=kOutput, calls=%fused_computation.5 | convolution fusion | flops 3331129344 | bytes 7471104 | tf_op jit(solution)/shard_map/dot_general | solution.py:43
  74.7 6.9 %convolution_convert_fusion = bf16[768,768]{1,0:T(8,128)(2,1)} fusion(bf16[2048,768]{0,1:T(8,128)(2,1)} %add_convert_fusion.1), kind=kOutput, calls=%fused_computation.20 | convolution fusion | flops 2416508928 | bytes 4325376 | tf_op jit(solution)/shard_map/dot_general | solution.py:29
  81.5 8.5 %add_convert_fusion = bf16[2048,768]{0,1:T(8,128)(2,1)} fusion(bf16[2048,768]{0,1:T(8,128)(2,1)S(1)} %copy-done.5, bf16[768,768]{1,0:T(8,128)(2,1)} %convolution_convert_fusion), kind=kOutput, calls=%fused_computation.4 | convolution fusion | flops 3331129344 | bytes 7471104 | tf_op jit(solution)/shard_map/dot_general | solution.py:43
  90.0 3.2 %copy.37 = bf16[2048,768]{1,0:T(8,128)(2,1)S(1)} copy(bf16[2048,768]{0,1:T(8,128)(2,1)} %add_convert_fusion) | data formatting | bytes 6291456 | tf_op jit(solution)/shard_map/reshape | solution.py:117
  93.2 0.0 copy-start
  93.2 0.0 copy-start.1
  93.2 6.5 %all_to_all.20 = bf16[2,1024,768]{2,1,0:T(8,128)(2,1)S(1)} all-to-all(bf16[2,1024,768]{2,1,0:T(8,128)(2,1)S(1)} %bitcast.65), channel_id=1, replica_groups=mesh['ep'=16,'rep'=2] {'rep'}, dimensions={0} | all-to-all | bytes 6291456 | tf_op jit(solution)/shard_map/all_to_all | solution.py:116
  99.7 2.7 subtract_convert_fusion
  102.5 3.4 %reshape.128 = bf16[2,16,49152]{2,1,0:T(8,128)(2,1)S(1)} reshape(bf16[2,1024,768]{2,1,0:T(8,128)(2,1)} %subtract_convert_fusion) | data formatting | bytes 6291456 | tf_op jit(solution)/shard_map/reshape | solution.py:123
  105.9 4.9 %copy.34 = bf16[2,16,49152]{2,0,1:T(2,128)(2,1)} copy(bf16[2,16,49152]{2,1,0:T(8,128)(2,1)S(1)} %reshape.128) | data formatting | bytes 6291456 | tf_op jit(solution)/shard_map/reshape | solution.py:123
  110.8 5.9 %all-to-all-start.2 = ((bf16[2,16,49152]{2,0,1:T(2,128)(2,1)}), bf16[2,16,49152]{2,0,1:T(2,128)(2,1)S(1)}, u32[]{:S(2)}, u32[]{:S(2)}) async-start(bf16[2,16,49152]{2,0,1:T(2,128)(2,1)} %copy.34), calls=%async_computation.2 | async-start | bytes 6291456 | tf_op jit(solution)/shard_map/all_to_all | solution.py:122
  116.8 0.6 scatter_custom_fusion
  117.5 60.5 %all-to-all-done.2 = bf16[2,16,49152]{2,0,1:T(2,128)(2,1)S(1)} async-done(((bf16[2,16,49152]{2,0,1:T(2,128)(2,1)}), bf16[2,16,49152]{2,0,1:T(2,128)(2,1)S(1)}, u32[]{:S(2)}, u32[]{:S(2)}) %all-to-all-start.2) | async-done | bytes 3145760 | tf_op jit(solution)/shard_map/all_to_all | solution.py:122
  177.9 8.3 %gather_fusion = bf16[16,2,49152]{2,1,0:T(2,128)(2,1)} fusion(bf16[2,16,49152]{2,0,1:T(2,128)(2,1)S(1)} %all-to-all-done.2, s32[1024]{0:T(1024)S(1)} %pad_clamp_fusion), kind=kCustom, calls=%fused_computation | custom fusion | bytes 6291520 | tf_op jit(solution)/shard_map/jit(_take)/gather | solution.py:125
  186.3 4.7 %fusion.2 = bf16[2,16,49152]{2,0,1:T(2,128)(2,1)S(1)} fusion(bf16[16,2,49152]{2,1,0:T(2,128)(2,1)} %gather_fusion, pred[16]{0:T(512)(128)(4,1)S(1)} %compare_and_fusion), kind=kLoop, calls=%fused_computation.14 | loop fusion | flops 1572864 | bytes 6291472 | tf_op jit(solution)/shard_map/jit(_take)/select_n | solution.py:125
  190.9 86.2 %all_to_all.21 = bf16[2,16,49152]{2,0,1:T(2,128)(2,1)S(1)} all-to-all(bf16[2,16,49152]{2,0,1:T(2,128)(2,1)S(1)} %fusion.2), channel_id=1, replica_groups=mesh['ep'=16,'rep'=2] {'ep'}, dimensions={1} | all-to-all | bytes 6291456 | tf_op jit(solution)/shard_map/all_to_all | solution.py:126
  277.1 14.0 %slice_reduce_fusion = (bf16[16,49152]{1,0:T(8,128)(2,1)S(1)}, bf16[16,49152]{1,0:T(8,128)(2,1)S(1)}) fusion(bf16[2,16,49152]{2,0,1:T(2,128)(2,1)S(1)} %all_to_all.21), kind=kLoop, calls=%fused_computation.10 | loop fusion | bytes 6291456 | tf_op jit(solution)/shard_map/slice | solution.py:128
  291.1 1.6 slice.21
  292.7 1.6 slice.23
  (22 shorter events, 0.1 us)
Async XLA Ops:
  7.2 17.2 %copy-start.2 = (bf16[1,1,16,16,2048]{4,3,2,1,0:T(8,128)(2,1)S(1)}, bf16[1,1,16,16,2048]{4,3,2,1,0:T(8,128)(2,1)}, u32[]{:S(2)}) copy-start(bf16[1,1,16,16,2048]{4,3,2,1,0:T(8,128)(2,1)} %param.15) | copy-start | bytes 3145732
  7.2 41.5 %copy-start.3 = (bf16[1,1,16,16,768]{4,3,2,1,0:T(8,128)(2,1)S(1)}, bf16[1,1,16,16,768]{4,3,2,1,0:T(8,128)(2,1)}, u32[]{:S(2)}) copy-start(bf16[1,1,16,16,768]{4,3,2,1,0:T(8,128)(2,1)} %param.16) | copy-start | bytes 1179652
  7.2 41.5 %all-gather.3.cloned.1.call-start = ((), (), s32[]{:S(2)}) async-start(), calls=%async_computation.4 | async-start | bytes 4718592 | tf_op jit(solution)/shard_map/all_gather | solution.py:92
  15.9 32.8 %all-to-all-start = ((bf16[16,16,2048]{2,1,0:T(8,128)(2,1)}), bf16[16,16,2048]{2,1,0:T(8,128)(2,1)S(1)}, u32[]{:S(2)}, u32[]{:S(2)}) async-start(bf16[16,16,2048]{2,1,0:T(8,128)(2,1)} %bitcast.4), calls=%async_computation | async-start | bytes 2097152 | tf_op jit(solution)/shard_map/all_to_all | solution.py:86
  24.4 28.8 %collective-permute-start.1 = (bf16[256,2048]{1,0:T(8,128)(2,1)S(1)}, bf16[256,2048]{1,0:T(8,128)(2,1)S(1)}, u32[]{:S(2)}, u32[]{:S(2)}) collective-permute-start(bf16[256,2048]{1,0:T(8,128)(2,1)S(1)} %bitcast.70), channel_id=1, source_target_pairs={{0,1},{1,0},{2,3},{3,2},{4,5},{5,4},{6,7},{7,6},{8,9},{9,8},{10,11... | collective-permute-start | bytes 3145736 | tf_op jit(solution)/shard_map/ppermute | solution.py:25
  52.0 1.8 collective-permute-start
  74.7 6.9 %copy-start.5 = (bf16[2048,768]{0,1:T(8,128)(2,1)S(1)}, bf16[2048,768]{0,1:T(8,128)(2,1)}, u32[]{:S(2)}) copy-start(bf16[2048,768]{0,1:T(8,128)(2,1)} %add_convert_fusion.1) | copy-start | bytes 9437188
  93.2 6.6 %copy-start = (bf16[1,1024,768]{2,1,0:T(8,128)(2,1)S(1)}, bf16[1,1024,768]{2,1,0:T(8,128)(2,1)}, u32[]{:S(2)}) copy-start(bf16[1,1024,768]{2,1,0:T(8,128)(2,1)} %param.20) | copy-start | bytes 4718596
  93.2 6.5 %copy-start.1 = (bf16[1,1024,768]{2,1,0:T(8,128)(2,1)S(1)}, bf16[1,1024,768]{2,1,0:T(8,128)(2,1)}, u32[]{:S(2)}) copy-start(bf16[1,1024,768]{2,1,0:T(8,128)(2,1)} %param.19) | copy-start | bytes 4718596
  110.8 6.0 %copy-start.4 = (s32[16]{0:T(128)S(1)}, s32[16]{0:T(128)}, u32[]{:S(2)}) copy-start(s32[16]{0:T(128)} %param.21) | copy-start | bytes 196
  110.8 67.1 %all-to-all-start.2 = ((bf16[2,16,49152]{2,0,1:T(2,128)(2,1)}), bf16[2,16,49152]{2,0,1:T(2,128)(2,1)S(1)}, u32[]{:S(2)}, u32[]{:S(2)}) async-start(bf16[2,16,49152]{2,0,1:T(2,128)(2,1)} %copy.34), calls=%async_computation.2 | async-start | bytes 6291456 | tf_op jit(solution)/shard_map/all_to_all | solution.py:122
Sparse Core Ops, SparseCore 0:
  9.6 14.8 all-gather.2
where the time goes:
time: 305 us; the launch traced here: 302 us
  blocking collectives  92.7 us (30%)
  waiting for transfers between devices  86 us (28%)
  local copies, waits for them, and re-layouts  39.4 us (13%)
  matrix products  36.2 us (12%)
  other arithmetic  17.4 us (6%)
  between operations  15.4 us (5%)
  starting transfers between devices  14.6 us (5%)
    all_to_all x1, blocking collectives, shards(): lax.all_to_all(arranged, 'ep', split_axis=1, concat_axis=1, tiled=True)  86.2 us
    all_to_all x1, waiting for transfers between devices, shards(): lax.all_to_all(updated.reshape(2, experts, -1), 'ep', split_axis=1, conca...  60.5 us
    all_to_all x1, waiting for transfers between devices, shards(): lax.all_to_all(outgoing.reshape(experts, capacity, width), 'ep', split_ax...  24.2 us
    slice x3, local copies, waits for them, and re-layouts, shards(): return (result[0:1], result[1:2])  17.2 us
    dot_general x2, matrix products, orthogonalize(): jnp.dot(iterate, poly, preferred_element_type=jnp.float32)  16.9 us
    dot_general x4, matrix products, contract_rows(): lax.dot_general(left, right, (((0,), (0,)), ((), ())), preferred_element_...  16 us
    all_to_all x1, starting transfers between devices, shards(): lax.all_to_all(outgoing.reshape(experts, capacity, width), 'ep', split_ax...  8.48 us
    reshape x2, local copies, waits for them, and re-layouts, shards(): updated.reshape(2, experts, -1)  8.33 us
  transfers between devices with their start and end apart: 5, of which 3 were waited for; matrix products, arithmetic and copies ran while one was open for 4% of the time, Pallas kernels for 0%

commit v1 on v0

v1 whole, which is shorter than its diff:
```python
import functools
import math

import jax
import jax.numpy as jnp
from jax import lax
from jax.experimental import pallas as pl
from jax.experimental.pallas import tpu as pltpu
from jax.sharding import PartitionSpec as P

ITERS = 2

quintic_first = 3.4445
quintic_second = -4.775
quintic_third = 2.0315
step_scale = 2.0
epsilon = 1e-07

VMEM = pl.BlockSpec(memory_space=pltpu.VMEM)
SMEM = pl.BlockSpec(memory_space=pltpu.SMEM)
ANY = pl.BlockSpec(memory_space=pl.ANY)
MIB = 1 << 20


def from_partner(block):
    return lax.ppermute(block, "rep", [(0, 1), (1, 0)])


def mm(left, right, dims=((1,), (0,))):
    return lax.dot_general(left, right, (dims, ((), ())), preferred_element_type=jnp.float32)


def call(kernel, outs, in_specs, args, flops, nbytes, scratch=(), limit=40):
    return pl.pallas_call(
        kernel,
        out_shape=outs,
        in_specs=in_specs,
        out_specs=jax.tree.map(lambda _: VMEM, outs),
        scratch_shapes=list(scratch),
        compiler_params=pltpu.CompilerParams(vmem_limit_bytes=limit * MIB),
        cost_estimate=pl.CostEstimate(flops=flops, bytes_accessed=nbytes, transcendentals=0),
    )(*args)


def dispatch_kernel(capacity, rep_ref, ids_ref, copy_ref, probs_ref, dy_ref, out_ref):
    rows, tokens = out_ref.shape[0], dy_ref.shape[0]
    own = rep_ref[0]
    expert = lax.broadcasted_iota(jnp.int32, (rows, tokens), 0) // capacity
    slot = lax.broadcasted_iota(jnp.int32, (rows, tokens), 0) % capacity
    mask = jnp.zeros((rows, tokens), jnp.float32)
    weight = jnp.zeros((rows, tokens), jnp.float32)
    for k in range(ids_ref.shape[0]):
        here = (ids_ref[k : k + 1, :] == expert) & (copy_ref[k : k + 1, :] == own)
        mask = jnp.where(here, 1.0, mask)
        weight = jnp.where(here, probs_ref[k : k + 1, :], weight)
    before = lax.broadcasted_iota(jnp.int32, (tokens, tokens), 0) < lax.broadcasted_iota(
        jnp.int32, (tokens, tokens), 1
    )
    rank = mm(mask.astype(jnp.bfloat16), jnp.where(before, 1.0, 0.0).astype(jnp.bfloat16))
    hot = (mask > 0.5) & (rank.astype(jnp.int32) == slot)
    scale = jnp.sum(jnp.where(hot, weight, 0.0), axis=1, keepdims=True)
    picked = mm(jnp.where(hot, 1.0, 0.0).astype(jnp.bfloat16), dy_ref[...])
    out_ref[...] = (picked * scale).astype(jnp.bfloat16)


def inputs_kernel(rep_ref, own_ref, other_ref, high_ref, low_ref, xt_ref):
    half = xt_ref.shape[0]
    rows = own_ref.shape[0]
    own, other = own_ref[...], other_ref[...]

    def store(first, second, block):
        high = block.astype(jnp.bfloat16)
        high_ref[first, second] = high
        low_ref[first, second] = (block - high.astype(jnp.float32)).astype(jnp.bfloat16)

    begin, end = slice(0, rows), slice(rows, None)
    store(begin, begin, mm(own, own, ((1,), (1,))))
    store(end, end, mm(other, other, ((1,), (1,))))
    cross = mm(own, other, ((1,), (1,)))
    store(begin, end, cross)
    store(end, begin, cross.T)
    start = pl.multiple_of(rep_ref[0] * half, half)
    xt_ref[:, :rows] = own_ref[:, pl.ds(start, half)].T
    xt_ref[:, rows:] = other_ref[:, pl.ds(start, half)].T


def rows_kernel(
    rep_ref, routed_ref, own_down_ref, other_down_ref, gate_ref, up_ref, own_ref, partner_ref
):
    half = own_down_ref.shape[1]
    inner = own_down_ref.shape[0]
    rep = rep_ref[0]
    first = pl.multiple_of(rep * half, half)
    second = pl.multiple_of((1 - rep) * half, half)
    hidden = mm(routed_ref[:, pl.ds(first, half)], own_down_ref[...], ((1,), (1,)))
    hidden += mm(routed_ref[:, pl.ds(second, half)], other_down_ref[...], ((1,), (1,)))
    hidden = hidden / math.sqrt(inner)
    gate = gate_ref[...].astype(jnp.float32)
    up = up_ref[...].astype(jnp.float32)
    sigmoid = 1.0 / (1.0 + jnp.exp(-gate))
    gate_rows = (hidden * up * sigmoid * (1.0 + gate * (1.0 - sigmoid))).astype(jnp.bfloat16)
    up_rows = (hidden * gate * sigmoid).astype(jnp.bfloat16)

    @pl.when(rep == 0)
    def _():
        own_ref[...] = gate_rows
        partner_ref[...] = up_rows

    @pl.when(rep == 1)
    def _():
        own_ref[...] = up_rows
        partner_ref[...] = gate_rows


def schulz_kernel(own_ref, other_ref, high_ref, low_ref, b_ref, r_ref, gram_ref, poly_ref):
    rows = own_ref.shape[0]
    r_ref[:rows] = own_ref[...]
    r_ref[rows:] = other_ref[...]
    size = None
    for repeat in range(ITERS):
        base = r_ref[...]
        mapped = mm(high_ref[...], base) + mm(low_ref[...], base)
        if repeat == 0:
            squares = jnp.sum(base.astype(jnp.float32) * mapped)
            total = jnp.sqrt(jnp.maximum(squares, 0.0)) + epsilon
            size = 1.0 / total
        gram = mm(base, mapped.astype(jnp.bfloat16), ((0,), (0,)))
        if repeat == 0:
            gram = gram * (size * size)
        gram_ref[...] = gram.astype(jnp.bfloat16)
        square = mm(gram_ref[...], gram_ref[...])
        poly_ref[...] = (
            quintic_second * gram_ref[...].astype(jnp.float32) + quintic_third * square
        ).astype(jnp.bfloat16)
        mixed = quintic_first * base.astype(jnp.float32) + mm(base, poly_ref[...])
        if repeat == 0:
            mixed = mixed * size
        if repeat == ITERS - 1:
            b_ref[...] = mixed.astype(jnp.bfloat16)
        else:
            r_ref[...] = mixed.astype(jnp.bfloat16)


def update_kernel(factor, rep_ref, own_ref, other_ref, xt_ref, gate_ref, up_ref, gate_out, up_out):
    rows = own_ref.shape[0] // 2
    rep = rep_ref[0]

    def update(weight_ref, out_ref, swapped):
        b_ref = other_ref if swapped else own_ref
        first, second = (slice(rows, None), slice(0, rows)) if swapped else (slice(0, rows), slice(rows, None))
        ortho = mm(xt_ref[:, :rows], b_ref[first]) + mm(xt_ref[:, rows:], b_ref[second])
        out_ref[...] = (weight_ref[...].astype(jnp.float32) - factor * ortho).astype(jnp.bfloat16)

    @pl.when(rep == 0)
    def _():
        update(gate_ref, gate_out, False)
        update(up_ref, up_out, True)

    @pl.when(rep == 1)
    def _():
        update(gate_ref, gate_out, True)
        update(up_ref, up_out, False)


def arrange_kernel(index_ref, in_ref, out_ref, sems):
    count = in_ref.shape[0]
    copies = [
        pltpu.make_async_copy(in_ref.at[index_ref[i]], out_ref.at[i], sems.at[i])
        for i in range(count)
    ]
    for copy in copies:
        copy.start()
    for copy in copies:
        copy.wait()


def arrange(blocks, index):
    return pl.pallas_call(
        arrange_kernel,
        out_shape=jax.ShapeDtypeStruct(blocks.shape, blocks.dtype),
        in_specs=[SMEM, ANY],
        out_specs=ANY,
        scratch_shapes=[pltpu.SemaphoreType.DMA((blocks.shape[0],))],
        cost_estimate=pl.CostEstimate(
            flops=0, bytes_accessed=4 * blocks.size, transcendentals=0
        ),
    )(index, blocks)


def exchange(blocks):
    return lax.all_to_all(blocks, "ep", split_axis=0, concat_axis=0, tiled=True)


def shards(
    dy,
    probs,
    expert_ids,
    copy_choice,
    saved_inputs,
    saved_gate,
    saved_up,
    down_weight,
    gate_weight,
    up_weight,
    new_owner,
):
    experts = lax.axis_size("ep")
    capacity = saved_inputs.shape[3]
    width = dy.shape[1]
    inner = saved_gate.shape[4]
    half = width // 2
    rows = experts * capacity
    bf16 = jnp.bfloat16
    shape = lambda *dims: jax.ShapeDtypeStruct(dims, bf16)
    rep = lax.axis_index("rep").astype(jnp.int32).reshape(1)

    outgoing = call(
        functools.partial(dispatch_kernel, capacity),
        shape(rows, width),
        [SMEM, VMEM, VMEM, VMEM, VMEM],
        (rep, expert_ids.T, copy_choice.T, probs.T, dy),
        2 * rows * dy.shape[0] * width,
        2 * rows * width,
    )
    routed = exchange(outgoing.reshape(experts, capacity, width)).reshape(rows, width)

    inputs = saved_inputs.reshape(rows, width)
    down = down_weight[0]
    other_inputs = from_partner(inputs)
    other_down = from_partner(down)
    high, low, transposed = call(
        inputs_kernel,
        (shape(2 * rows, 2 * rows), shape(2 * rows, 2 * rows), shape(half, 2 * rows)),
        [SMEM, VMEM, VMEM],
        (rep, inputs, other_inputs),
        2 * 3 * rows * rows * width,
        8 * rows * width,
    )
    own_rows, partner_rows = call(
        rows_kernel,
        (shape(rows, inner), shape(rows, inner)),
        [SMEM] + [VMEM] * 5,
        (rep, routed, down, other_down, saved_gate.reshape(rows, inner), saved_up.reshape(rows, inner)),
        2 * rows * width * inner,
        2 * inner * width,
    )
    other_rows = from_partner(partner_rows)
    own_b = call(
        schulz_kernel,
        shape(2 * rows, inner),
        [VMEM] * 4,
        (own_rows, other_rows, high, low),
        ITERS * 2 * inner * inner * (inner + 6 * rows),
        8 * rows * inner,
        scratch=(
            pltpu.VMEM((2 * rows, inner), bf16),
            pltpu.VMEM((inner, inner), bf16),
            pltpu.VMEM((inner, inner), bf16),
        ),
    )
    other_b = from_partner(own_b)
    gate, up = call(
        functools.partial(update_kernel, step_scale * math.sqrt(width)),
        (shape(half, inner), shape(half, inner)),
        [SMEM] + [VMEM] * 5,
        (rep, own_b, other_b, transposed, gate_weight[0], up_weight[0]),
        2 * 2 * half * 2 * rows * inner,
        8 * half * inner,
    )
    place = jnp.arange(experts, dtype=jnp.int32)
    source = jnp.sum(
        jnp.where(new_owner[None, :] == place[:, None], place[None, :], 0), axis=1, dtype=jnp.int32
    )
    pieces = (experts, half // experts, inner)
    results = []
    for matrix in (gate, up):
        spread = exchange(matrix.reshape(pieces))
        results.append(spread)
    results = [exchange(arrange(spread, source)).reshape(1, half, inner) for spread in results]
    return tuple(results)


def solution(mesh):
    in_specs = (
        P("ep", None),
        P("ep", None),
        P("ep", None),
        P("ep", None),
        P("ep", "rep", None, None, None),
        P("ep", "rep", None, None, None),
        P("ep", "rep", None, None, None),
        P("ep", None, "rep"),
        P("ep", "rep", None),
        P("ep", "rep", None),
        P(),
    )
    out_specs = (P("ep", "rep", None), P("ep", "rep", None))
    return jax.shard_map(shards, mesh=mesh, in_specs=in_specs, out_specs=out_specs, check_vma=False)
```

time: 305 us -> 255 us (0.84)
  Pallas kernels: 0 us -> 114 us
  blocking collectives: 92.7 us -> 43.6 us
  matrix products: 36.2 us -> 0 us
  local copies, waits for them, and re-layouts: 39.4 us -> 8.96 us
  waiting for transfers between devices: 86 us -> 57.2 us
  other arithmetic: 17.4 us -> 0.64 us
  between operations: 15.4 us -> 0.82 us
  starting transfers between devices: 14.6 us -> 27.4 us
    pallas_call x0 -> x7, Pallas kernels: none -> 114 us  [the longest x2 99.1 us: arrange(): pl.pallas_call(arrange_kernel, out_shape=jax.ShapeDtypeStruct(blocks.shap...]
    all_to_all x2 -> x1, blocking collectives: 92.7 us -> 43.6 us  [exchange(): return lax.all_to_all(blocks, 'ep', split_axis=0, concat_axis=0, tiled=True)]
    dot_general x7 -> x0, matrix products: 36.2 us -> none  [the longest x2 16.9 us: orthogonalize(): jnp.dot(iterate, poly, preferred_element_type=jnp.float32)]
    all_to_all x2 -> x4, waiting for transfers between devices: 84.7 us -> 50.9 us  [exchange(): return lax.all_to_all(blocks, 'ep', split_axis=0, concat_axis=0, tiled=True)]
    slice x4 -> x0, local copies, waits for them, and re-layouts: 17.4 us -> none  [the longest x3 17.2 us: shards(): return (result[0:1], result[1:2])]
    all_to_all x2 -> x4, starting transfers between devices: 14.4 us -> 26.2 us  [exchange(): return lax.all_to_all(blocks, 'ep', split_axis=0, concat_axis=0, tiled=True)]
    reshape x3 -> x0, local copies, waits for them, and re-layouts: 11.5 us -> none  [the longest x2 8.33 us: shards(): updated.reshape(2, experts, -1)]
    gather x1 -> x0, local copies, waits for them, and re-layouts: 8.33 us -> none  [shards(): arranged = jnp.take(spread_out, inverse, axis=1)]
  transfers between devices with their start and end apart: 5 -> 8, of which waited for: 3 -> 4; matrix products, arithmetic and copies ran while one was open for 4% -> 0% of each run, Pallas kernels for 0% -> 41%
where the time goes in v1:
time: 255 us; the launch traced here: 253 us
  Pallas kernels  114 us (45%)
  waiting for transfers between devices  57.2 us (22%)
  blocking collectives  43.6 us (17%)
  starting transfers between devices  27.4 us (11%)
  local copies, waits for them, and re-layouts  8.96 us (4%)
    pallas_call x2, Pallas kernels, arrange(): pl.pallas_call(arrange_kernel, out_shape=jax.ShapeDtypeStruct(blocks.shap...  99.1 us
    all_to_all x4, waiting for transfers between devices, exchange(): return lax.all_to_all(blocks, 'ep', split_axis=0, concat_axis=0, tiled=True)  50.9 us
    all_to_all x1, blocking collectives, exchange(): return lax.all_to_all(blocks, 'ep', split_axis=0, concat_axis=0, tiled=True)  43.6 us
    all_to_all x4, starting transfers between devices, exchange(): return lax.all_to_all(blocks, 'ep', split_axis=0, concat_axis=0, tiled=True)  26.2 us
    pallas_call x5, Pallas kernels, call(): pl.pallas_call(kernel, out_shape=outs, in_specs=in_specs, out_specs=jax.t...  15.3 us
    unnamed x30, local copies, waits for them, and re-layouts  8.96 us
    ppermute x4, waiting for transfers between devices, from_partner(): return lax.ppermute(block, 'rep', [(0, 1), (1, 0)])  6.28 us
  transfers between devices with their start and end apart: 8, of which 4 were waited for; matrix products, arithmetic and copies ran while one was open for 0% of the time, Pallas kernels for 41%

profile of v1, /device:TPU:0, one launch (start us, length us, event | category | flops | bytes accessed | tf_op | source)
XLA Modules:
  0.0 253.0 jit_solution(14371975049622320197)
XLA Ops:
  0.6 0.0 copy-start.5
  0.6 0.9 copy-done.5
  1.5 0.0 copy-start.6
  1.5 0.7 copy-done.6
  2.2 0.0 copy-start.7
  2.2 0.7 copy-done.7
  2.9 0.0 copy-start.8
  2.9 0.7 copy-done.8
  3.6 1.6 shard_map.122
  5.3 8.3 %all-to-all-start = ((bf16[16,16,2048]{2,1,0:T(8,128)(2,1)}), bf16[16,16,2048]{2,1,0:T(8,128)(2,1)S(1)}, u32[]{:S(2)}, u32[]{:S(2)}) async-start(bf16[16,16,2048]{2,1,0:T(8,128)(2,1)} %bitcast.4), calls=%async_computation | async-start | bytes 2097152 | tf_op jit(solution)/shard_map/all_to_all | solution.py:191
  13.6 0.0 copy-done
  13.6 0.1 collective-permute-start
  13.7 0.5 collective-permute-start.2
  14.2 4.4 %collective-permute-done.other_down_ref = bf16[768,1024]{1,0:T(8,128)(2,1)S(1)} collective-permute-done((bf16[768,1024]{1,0:T(8,128)(2,1)S(1)}, bf16[768,1024]{1,0:T(8,128)(2,1)S(1)}, u32[]{:S(2)}, u32[]{:S(2)}) %collective-permute-start) | collective-permute-done | bytes 1572896 | tf_op jit(solution)/shard_map/ppermute | solution.py:26
  18.5 1.1 copy-done.1
  19.7 18.4 %all-to-all-done = bf16[16,16,2048]{2,1,0:T(8,128)(2,1)S(1)} async-done(((bf16[16,16,2048]{2,1,0:T(8,128)(2,1)}), bf16[16,16,2048]{2,1,0:T(8,128)(2,1)S(1)}, u32[]{:S(2)}, u32[]{:S(2)}) %all-to-all-start) | async-done | bytes 1048608 | tf_op jit(solution)/shard_map/all_to_all | solution.py:191
  38.0 0.0 copy-done.3
  38.0 0.0 copy-done.4
  38.0 1.4 copy-done.2
  39.4 1.3 shard_map.123
  40.7 0.1 collective-permute-start.1
  40.8 0.0 collective-permute-done.2.other_ref
  40.8 0.0 copy-done.11
  40.8 2.3 shard_map.124
  43.2 0.0 collective-permute-done.1.other_ref
  43.2 0.0 copy-start.9
  43.2 0.0 copy-start.10
  43.2 6.9 %shard_map.125.own_ref = bf16[512,768]{1,0:T(8,128)(2,1)S(1)} custom-call(bf16[256,768]{1,0:T(8,128)(2,1)S(1)} %get-tuple-element.9.own_ref, bf16[256,768]{1,0:T(8,128)(2,1)S(1)} %collective-permute-done.1.other_ref, bf16[512,512]{1,0:T(8,128)(2,1)S(1)} %get-tuple-element.11.high_ref, bf16[512,512]{1,0:T(8,128)(2,1)S(1)} %get-tuple-element.12.low_ref), custom_call_target="tpu_custom_call" | custom-call | flops 5435817984 | bytes 1572864 | tf_op jit(solution)/shard_map/pallas_call | solution.py:34
  50.1 0.5 collective-permute-start.3
  50.6 1.9 collective-permute-done.3.other_ref
  52.5 0.0 copy-done.9
  52.5 0.0 copy-done.10
  52.5 3.1 %shard_map.126 = (bf16[1024,768]{1,0:T(8,128)(2,1)}, bf16[1024,768]{1,0:T(8,128)(2,1)S(1)}) custom-call(s32[1]{0:T(128)} %bitcast.rep_ref, bf16[512,768]{1,0:T(8,128)(2,1)S(1)} %shard_map.125.own_ref, bf16[512,768]{1,0:T(8,128)(2,1)S(1)} %collective-permute-done.3.other_ref, bf16[1024,512]{1,0:T(8,128)(2,1)S(1)} %get-tuple-element.13.xt_ref, ...), custom_call_target="tpu_custom_call" | custom-call | flops 1610612736 | bytes 6291456 | tf_op jit(solution)/shard_map/pallas_call | solution.py:34
  55.7 43.6 %all_to_all.25.in_ref = bf16[16,64,768]{2,1,0:T(8,128)(2,1)} all-to-all(bf16[16,64,768]{2,1,0:T(8,128)(2,1)S(1)} %bitcast.19), channel_id=1, replica_groups=mesh['ep'=16,'rep'=2] {'ep'}, dimensions={0} | all-to-all | bytes 3145728 | tf_op jit(solution)/shard_map/all_to_all | solution.py:191
  99.3 4.1 %all-to-all-start.1 = ((bf16[16,64,768]{2,1,0:T(8,128)(2,1)}), bf16[16,64,768]{2,1,0:T(8,128)(2,1)S(1)}, u32[]{:S(2)}, u32[]{:S(2)}) async-start(bf16[16,64,768]{2,1,0:T(8,128)(2,1)} %bitcast.12), calls=%async_computation.1 | async-start | bytes 3145728 | tf_op jit(solution)/shard_map/all_to_all | solution.py:191
  103.4 0.0 copy-done.13
  103.4 0.6 select_reduce_fusion.index_ref
  104.0 49.6 %shard_map.128 = bf16[16,64,768]{2,1,0:T(8,128)(2,1)} custom-call(s32[16]{0:T(128)} %select_reduce_fusion.index_ref, bf16[16,64,768]{2,1,0:T(8,128)(2,1)} %all_to_all.25.in_ref), custom_call_target="tpu_custom_call" | custom-call | bytes 3145728 | tf_op jit(solution)/shard_map/pallas_call | solution.py:178
  153.6 0.0 all-to-all-done.1.in_ref
  153.6 0.0 copy-start.12
  153.6 1.1 copy-done.12
  154.8 6.9 %all-to-all-start.4 = ((bf16[16,64,768]{2,1,0:T(8,128)(2,1)}), bf16[16,64,768]{2,1,0:T(8,128)(2,1)S(1)}, u32[]{:S(2)}, u32[]{:S(2)}) async-start(bf16[16,64,768]{2,1,0:T(8,128)(2,1)} %shard_map.128), calls=%async_computation.4 | async-start | bytes 3145728 | tf_op jit(solution)/shard_map/all_to_all | solution.py:191
  161.7 49.6 %shard_map.127 = bf16[16,64,768]{2,1,0:T(8,128)(2,1)} custom-call(s32[16]{0:T(128)} %select_reduce_fusion.index_ref, bf16[16,64,768]{2,1,0:T(8,128)(2,1)} %copy-done.12), custom_call_target="tpu_custom_call" | custom-call | bytes 3145728 | tf_op jit(solution)/shard_map/pallas_call | solution.py:178
  211.2 0.0 all-to-all-done.4
  211.2 6.9 %all-to-all-start.2 = ((bf16[16,64,768]{2,1,0:T(8,128)(2,1)}), bf16[16,64,768]{2,1,0:T(8,128)(2,1)S(1)}, u32[]{:S(2)}, u32[]{:S(2)}) async-start(bf16[16,64,768]{2,1,0:T(8,128)(2,1)} %shard_map.127), calls=%async_computation.2 | async-start | bytes 3145728 | tf_op jit(solution)/shard_map/all_to_all | solution.py:191
  218.2 32.5 %all-to-all-done.2 = bf16[16,64,768]{2,1,0:T(8,128)(2,1)S(1)} async-done(((bf16[16,64,768]{2,1,0:T(8,128)(2,1)}), bf16[16,64,768]{2,1,0:T(8,128)(2,1)S(1)}, u32[]{:S(2)}, u32[]{:S(2)}) %all-to-all-start.2) | async-done | bytes 1572896 | tf_op jit(solution)/shard_map/all_to_all | solution.py:191
  250.7 1.1 copy.15
  251.8 1.1 copy.16
  (7 shorter events, 0.0 us)
Async XLA Ops:
  0.6 0.9 copy-start.5
  1.5 0.7 copy-start.6
  2.2 0.7 copy-start.7
  2.9 0.7 copy-start.8
  3.6 10.0 %copy-start = (bf16[1,768,1024]{2,1,0:T(8,128)(2,1)S(1)}, bf16[1,768,1024]{2,1,0:T(8,128)(2,1)}, u32[]{:S(2)}) copy-start(bf16[1,768,1024]{2,1,0:T(8,128)(2,1)} %param.18) | copy-start | bytes 4718596
  3.6 34.4 %copy-start.3 = (bf16[1,1,16,16,768]{4,3,2,1,0:T(8,128)(2,1)S(1)}, bf16[1,1,16,16,768]{4,3,2,1,0:T(8,128)(2,1)}, u32[]{:S(2)}) copy-start(bf16[1,1,16,16,768]{4,3,2,1,0:T(8,128)(2,1)} %param.16) | copy-start | bytes 1179652
  3.6 34.4 %copy-start.4 = (bf16[1,1,16,16,768]{4,3,2,1,0:T(8,128)(2,1)S(1)}, bf16[1,1,16,16,768]{4,3,2,1,0:T(8,128)(2,1)}, u32[]{:S(2)}) copy-start(bf16[1,1,16,16,768]{4,3,2,1,0:T(8,128)(2,1)} %param.17) | copy-start | bytes 1179652
  5.3 32.8 %all-to-all-start = ((bf16[16,16,2048]{2,1,0:T(8,128)(2,1)}), bf16[16,16,2048]{2,1,0:T(8,128)(2,1)S(1)}, u32[]{:S(2)}, u32[]{:S(2)}) async-start(bf16[16,16,2048]{2,1,0:T(8,128)(2,1)} %bitcast.4), calls=%async_computation | async-start | bytes 2097152 | tf_op jit(solution)/shard_map/all_to_all | solution.py:191
  13.6 4.9 %collective-permute-start = (bf16[768,1024]{1,0:T(8,128)(2,1)S(1)}, bf16[768,1024]{1,0:T(8,128)(2,1)S(1)}, u32[]{:S(2)}, u32[]{:S(2)}) collective-permute-start(bf16[768,1024]{1,0:T(8,128)(2,1)S(1)} %bitcast.17), channel_id=1, source_target_pairs={{0,1},{1,0},{2,3},{3,2},{4,5},{5,4},{6,7},{7,6},{8,9},{9,8},{10,11... | collective-permute-start | bytes 4718600 | tf_op jit(solution)/shard_map/ppermute | solution.py:26
  13.7 27.1 %collective-permute-start.2 = (bf16[256,2048]{1,0:T(8,128)(2,1)}, bf16[256,2048]{1,0:T(8,128)(2,1)}, u32[]{:S(2)}, u32[]{:S(2)}) collective-permute-start(bf16[256,2048]{1,0:T(8,128)(2,1)} %bitcast.27), channel_id=1, source_target_pairs={{0,1},{1,0},{2,3},{3,2},{4,5},{5,4},{6,7},{7,6},{8,9},{9,8},{10,11... | collective-permute-start | bytes 3145736 | tf_op jit(solution)/shard_map/ppermute | solution.py:26
  18.5 1.1 copy-start.1
  38.0 1.4 copy-start.2
  39.4 1.4 copy-start.11
  40.7 2.4 collective-permute-start.1
  43.2 9.4 %copy-start.9 = (bf16[1,1024,768]{2,1,0:T(8,128)(2,1)S(1)}, bf16[1,1024,768]{2,1,0:T(8,128)(2,1)}, u32[]{:S(2)}) copy-start(bf16[1,1024,768]{2,1,0:T(8,128)(2,1)} %param.19) | copy-start | bytes 4718596
  43.2 9.4 %copy-start.10 = (bf16[1,1024,768]{2,1,0:T(8,128)(2,1)S(1)}, bf16[1,1024,768]{2,1,0:T(8,128)(2,1)}, u32[]{:S(2)}) copy-start(bf16[1,1024,768]{2,1,0:T(8,128)(2,1)} %param.20) | copy-start | bytes 4718596
  50.1 2.5 collective-permute-start.3
  99.3 4.1 %copy-start.13 = (s32[16]{0:T(128)S(1)}, s32[16]{0:T(128)}, u32[]{:S(2)}) copy-start(s32[16]{0:T(128)} %param.21) | copy-start | bytes 196
  99.3 54.3 %all-to-all-start.1 = ((bf16[16,64,768]{2,1,0:T(8,128)(2,1)}), bf16[16,64,768]{2,1,0:T(8,128)(2,1)S(1)}, u32[]{:S(2)}, u32[]{:S(2)}) async-start(bf16[16,64,768]{2,1,0:T(8,128)(2,1)} %bitcast.12), calls=%async_computation.1 | async-start | bytes 3145728 | tf_op jit(solution)/shard_map/all_to_all | solution.py:191
  153.6 1.1 copy-start.12
  154.8 56.5 %all-to-all-start.4 = ((bf16[16,64,768]{2,1,0:T(8,128)(2,1)}), bf16[16,64,768]{2,1,0:T(8,128)(2,1)S(1)}, u32[]{:S(2)}, u32[]{:S(2)}) async-start(bf16[16,64,768]{2,1,0:T(8,128)(2,1)} %shard_map.128), calls=%async_computation.4 | async-start | bytes 3145728 | tf_op jit(solution)/shard_map/all_to_all | solution.py:191
  211.2 39.5 %all-to-all-start.2 = ((bf16[16,64,768]{2,1,0:T(8,128)(2,1)}), bf16[16,64,768]{2,1,0:T(8,128)(2,1)S(1)}, u32[]{:S(2)}, u32[]{:S(2)}) async-start(bf16[16,64,768]{2,1,0:T(8,128)(2,1)} %shard_map.127), calls=%async_computation.2 | async-start | bytes 3145728 | tf_op jit(solution)/shard_map/all_to_all | solution.py:191

commit v2 on v1

--- a/solution.py
+++ b/solution.py
@@ -18,7 +18,6 @@
 
 VMEM = pl.BlockSpec(memory_space=pltpu.VMEM)
 SMEM = pl.BlockSpec(memory_space=pltpu.SMEM)
-ANY = pl.BlockSpec(memory_space=pl.ANY)
 MIB = 1 << 20
 
 
@@ -162,29 +161,21 @@
         update(up_ref, up_out, False)
 
 
-def arrange_kernel(index_ref, in_ref, out_ref, sems):
-    count = in_ref.shape[0]
-    copies = [
-        pltpu.make_async_copy(in_ref.at[index_ref[i]], out_ref.at[i], sems.at[i])
-        for i in range(count)
-    ]
-    for copy in copies:
-        copy.start()
-    for copy in copies:
-        copy.wait()
+def arrange_kernel(index_ref, in_ref, out_ref):
+    for i in range(in_ref.shape[0]):
+        out_ref[i] = in_ref[index_ref[i]]
 
 
 def arrange(blocks, index):
-    return pl.pallas_call(
+    return call(
         arrange_kernel,
-        out_shape=jax.ShapeDtypeStruct(blocks.shape, blocks.dtype),
-        in_specs=[SMEM, ANY],
-        out_specs=ANY,
-        scratch_shapes=[pltpu.SemaphoreType.DMA((blocks.shape[0],))],
-        cost_estimate=pl.CostEstimate(
-            flops=0, bytes_accessed=4 * blocks.size, transcendentals=0
-        ),
-    )(index, blocks)
+        jax.ShapeDtypeStruct(blocks.shape, blocks.dtype),
+        [SMEM, VMEM],
+        (index, blocks),
+        0,
+        4 * blocks.size,
+        limit=16,
+    )
 
 
 def exchange(blocks):
@@ -214,14 +205,15 @@
     shape = lambda *dims: jax.ShapeDtypeStruct(dims, bf16)
     rep = lax.axis_index("rep").astype(jnp.int32).reshape(1)
 
-    outgoing = call(
+    outgoing = pl.pallas_call(
         functools.partial(dispatch_kernel, capacity),
-        shape(rows, width),
-        [SMEM, VMEM, VMEM, VMEM, VMEM],
-        (rep, expert_ids.T, copy_choice.T, probs.T, dy),
-        2 * rows * dy.shape[0] * width,
-        2 * rows * width,
-    )
+        out_shape=shape(rows, width),
+        grid=(1,),
+        in_specs=[SMEM]
+        + [pl.BlockSpec(a.shape, lambda i: (0, 0)) for a in (expert_ids.T, copy_choice.T, probs.T, dy)],
+        out_specs=pl.BlockSpec((rows, width), lambda i: (0, 0)),
+        compiler_params=pltpu.CompilerParams(vmem_limit_bytes=16 * MIB),
+    )(rep, expert_ids.T, copy_choice.T, probs.T, dy)
     routed = exchange(outgoing.reshape(experts, capacity, width)).reshape(rows, width)
 
     inputs = saved_inputs.reshape(rows, width)

time: 255 us -> 224 us (0.88)
  Pallas kernels: 114 us -> 17.8 us
  waiting for transfers between devices: 57.2 us -> 122 us
    pallas_call x2 -> x1, Pallas kernels: 99.1 us -> 1.65 us  [shards(): pl.pallas_call(functools.partial(dispatch_kernel, capacity), out_shape=sh...]
    all_to_all x4, waiting for transfers between devices: 50.9 us -> 116 us  [exchange(): return lax.all_to_all(blocks, 'ep', split_axis=0, concat_axis=0, tiled=True)]
    pallas_call x5 -> x6, Pallas kernels: 15.3 us -> 16.1 us  [call(): pl.pallas_call(kernel, out_shape=outs, in_specs=in_specs, out_specs=jax.t...]
  transfers between devices with their start and end apart: 8 -> 8, of which waited for: 4 -> 6; matrix products, arithmetic and copies ran while one was open for 0% -> 0% of each run, Pallas kernels for 41% -> 3%
where the time goes in v2:
time: 224 us; the launch traced here: 222 us
  waiting for transfers between devices  122 us (54%)
  blocking collectives  43.5 us (19%)
  starting transfers between devices  28.2 us (13%)
  Pallas kernels  17.8 us (8%)
  local copies, waits for them, and re-layouts  9.34 us (4%)
    all_to_all x4, waiting for transfers between devices, exchange(): return lax.all_to_all(blocks, 'ep', split_axis=0, concat_axis=0, tiled=True)  116 us
    all_to_all x1, blocking collectives, exchange(): return lax.all_to_all(blocks, 'ep', split_axis=0, concat_axis=0, tiled=True)  43.5 us
    all_to_all x4, starting transfers between devices, exchange(): return lax.all_to_all(blocks, 'ep', split_axis=0, concat_axis=0, tiled=True)  27 us
    pallas_call x6, Pallas kernels, call(): pl.pallas_call(kernel, out_shape=outs, in_specs=in_specs, out_specs=jax.t...  16.1 us
    unnamed x30, local copies, waits for them, and re-layouts  9.34 us
    ppermute x4, waiting for transfers between devices, from_partner(): return lax.ppermute(block, 'rep', [(0, 1), (1, 0)])  6.28 us
  transfers between devices with their start and end apart: 8, of which 6 were waited for; matrix products, arithmetic and copies ran while one was open for 0% of the time, Pallas kernels for 3%

profile of v2, /device:TPU:0, one launch (start us, length us, event | category | flops | bytes accessed | tf_op | source)
XLA Modules:
  0.0 221.5 jit_solution(10964579407381722579)
XLA Ops:
  0.6 0.0 copy-start.6
  0.6 0.9 copy-done.6
  1.5 0.0 copy-start.7
  1.5 0.7 copy-done.7
  2.2 0.0 copy-start.8
  2.2 0.7 copy-done.8
  2.9 0.0 copy-start.9
  2.9 0.7 copy-done.9
  3.6 1.6 shard_map.122
  5.3 8.3 %all-to-all-start = ((bf16[16,16,2048]{2,1,0:T(8,128)(2,1)}), bf16[16,16,2048]{2,1,0:T(8,128)(2,1)S(1)}, u32[]{:S(2)}, u32[]{:S(2)}) async-start(bf16[16,16,2048]{2,1,0:T(8,128)(2,1)} %bitcast.4), calls=%async_computation | async-start | bytes 2097152 | tf_op jit(solution)/shard_map/all_to_all | solution.py:182
  13.6 0.0 copy-done
  13.6 0.1 collective-permute-start
  13.7 0.5 collective-permute-start.2
  14.2 4.4 %collective-permute-done.other_down_ref = bf16[768,1024]{1,0:T(8,128)(2,1)S(1)} collective-permute-done((bf16[768,1024]{1,0:T(8,128)(2,1)S(1)}, bf16[768,1024]{1,0:T(8,128)(2,1)S(1)}, u32[]{:S(2)}, u32[]{:S(2)}) %collective-permute-start) | collective-permute-done | bytes 1572896 | tf_op jit(solution)/shard_map/ppermute | solution.py:25
  18.5 1.1 copy-done.1
  19.7 18.4 %all-to-all-done = bf16[16,16,2048]{2,1,0:T(8,128)(2,1)S(1)} async-done(((bf16[16,16,2048]{2,1,0:T(8,128)(2,1)}), bf16[16,16,2048]{2,1,0:T(8,128)(2,1)S(1)}, u32[]{:S(2)}, u32[]{:S(2)}) %all-to-all-start) | async-done | bytes 1048608 | tf_op jit(solution)/shard_map/all_to_all | solution.py:182
  38.0 0.0 copy-done.4
  38.0 0.0 copy-done.5
  38.0 1.4 copy-done.2
  39.4 1.3 shard_map.123
  40.7 0.1 collective-permute-start.1
  40.8 0.0 collective-permute-done.2.other_ref
  40.8 0.0 copy-done.12
  40.8 2.3 %shard_map.124 = (bf16[512,512]{1,0:T(8,128)(2,1)S(1)}, bf16[512,512]{1,0:T(8,128)(2,1)S(1)}, bf16[1024,512]{1,0:T(8,128)(2,1)S(1)}) custom-call(s32[1]{0:T(128)} %bitcast.rep_ref, bf16[256,2048]{1,0:T(8,128)(2,1)S(1)} %bitcast.29, bf16[256,2048]{1,0:T(8,128)(2,1)} %collective-permute-done.2.other_ref), custom_call_target="tpu_custom_call" | custom-call | flops 805306368 | bytes 4194304 | tf_op jit(solution)/shard_map/pallas_call | solution.py:33
  43.2 0.0 collective-permute-done.1.other_ref
  43.2 0.0 copy-start.10
  43.2 0.0 copy-start.11
  43.2 6.9 %shard_map.125.own_ref = bf16[512,768]{1,0:T(8,128)(2,1)S(1)} custom-call(bf16[256,768]{1,0:T(8,128)(2,1)S(1)} %get-tuple-element.9.own_ref, bf16[256,768]{1,0:T(8,128)(2,1)S(1)} %collective-permute-done.1.other_ref, bf16[512,512]{1,0:T(8,128)(2,1)S(1)} %get-tuple-element.11.high_ref, bf16[512,512]{1,0:T(8,128)(2,1)S(1)} %get-tuple-element.12.low_ref), custom_call_target="tpu_custom_call" | custom-call | flops 5435817984 | bytes 1572864 | tf_op jit(solution)/shard_map/pallas_call | solution.py:33
  50.1 0.6 collective-permute-start.3
  50.6 1.9 collective-permute-done.3.other_ref
  52.5 0.0 copy-done.10
  52.5 0.0 copy-done.11
  52.5 2.0 shard_map.126
  54.6 0.0 copy-start.3
  54.6 43.5 %all_to_all.25.in_ref = bf16[16,64,768]{2,1,0:T(8,128)(2,1)S(1)} all-to-all(bf16[16,64,768]{2,1,0:T(8,128)(2,1)S(1)} %bitcast.20), channel_id=1, replica_groups=mesh['ep'=16,'rep'=2] {'ep'}, dimensions={0} | all-to-all | bytes 3145728 | tf_op jit(solution)/shard_map/all_to_all | solution.py:182
  98.2 0.0 copy-done.3
  98.2 4.1 %all-to-all-start.1 = ((bf16[16,64,768]{2,1,0:T(8,128)(2,1)}), bf16[16,64,768]{2,1,0:T(8,128)(2,1)S(1)}, u32[]{:S(2)}, u32[]{:S(2)}) async-start(bf16[16,64,768]{2,1,0:T(8,128)(2,1)} %bitcast.19), calls=%async_computation.1 | async-start | bytes 3145728 | tf_op jit(solution)/shard_map/all_to_all | solution.py:182
  102.2 0.0 copy-done.13
  102.2 0.1 select_reduce_fusion.index_ref
  102.4 1.8 shard_map.128
  104.2 31.7 %all-to-all-done.1.in_ref = bf16[16,64,768]{2,1,0:T(8,128)(2,1)S(1)} async-done(((bf16[16,64,768]{2,1,0:T(8,128)(2,1)}), bf16[16,64,768]{2,1,0:T(8,128)(2,1)S(1)}, u32[]{:S(2)}, u32[]{:S(2)}) %all-to-all-start.1) | async-done | bytes 1572896 | tf_op jit(solution)/shard_map/all_to_all | solution.py:182
  135.9 7.3 %all-to-all-start.4 = ((bf16[16,64,768]{2,1,0:T(8,128)(2,1)}), bf16[16,64,768]{2,1,0:T(8,128)(2,1)}, u32[]{:S(2)}, u32[]{:S(2)}) async-start(bf16[16,64,768]{2,1,0:T(8,128)(2,1)} %shard_map.128), calls=%async_computation.4 | async-start | bytes 3145728 | tf_op jit(solution)/shard_map/all_to_all | solution.py:182
  143.2 1.8 shard_map.127
  145.0 31.9 %all-to-all-done.4 = bf16[16,64,768]{2,1,0:T(8,128)(2,1)} async-done(((bf16[16,64,768]{2,1,0:T(8,128)(2,1)}), bf16[16,64,768]{2,1,0:T(8,128)(2,1)}, u32[]{:S(2)}, u32[]{:S(2)}) %all-to-all-start.4) | async-done | bytes 1572896 | tf_op jit(solution)/shard_map/all_to_all | solution.py:182
  176.9 7.3 %all-to-all-start.2 = ((bf16[16,64,768]{2,1,0:T(8,128)(2,1)}), bf16[16,64,768]{2,1,0:T(8,128)(2,1)S(1)}, u32[]{:S(2)}, u32[]{:S(2)}) async-start(bf16[16,64,768]{2,1,0:T(8,128)(2,1)} %shard_map.127), calls=%async_computation.2 | async-start | bytes 3145728 | tf_op jit(solution)/shard_map/all_to_all | solution.py:182
  184.2 33.6 %all-to-all-done.2 = bf16[16,64,768]{2,1,0:T(8,128)(2,1)S(1)} async-done(((bf16[16,64,768]{2,1,0:T(8,128)(2,1)}), bf16[16,64,768]{2,1,0:T(8,128)(2,1)S(1)}, u32[]{:S(2)}, u32[]{:S(2)}) %all-to-all-start.2) | async-done | bytes 1572896 | tf_op jit(solution)/shard_map/all_to_all | solution.py:182
  217.7 1.1 copy.15
  218.9 2.7 %copy.16 = bf16[1,1024,768]{2,1,0:T(8,128)(2,1)} copy(bf16[1,1024,768]{2,1,0:T(8,128)(2,1)} %bitcast.15) | data formatting | bytes 3145728
  (7 shorter events, 0.0 us)
Async XLA Ops:
  0.6 0.9 copy-start.6
  1.5 0.7 copy-start.7
  2.2 0.7 copy-start.8
  2.9 0.7 copy-start.9
  3.6 10.0 %copy-start = (bf16[1,768,1024]{2,1,0:T(8,128)(2,1)S(1)}, bf16[1,768,1024]{2,1,0:T(8,128)(2,1)}, u32[]{:S(2)}) copy-start(bf16[1,768,1024]{2,1,0:T(8,128)(2,1)} %param.18) | copy-start | bytes 4718596
  3.6 34.4 %copy-start.4 = (bf16[1,1,16,16,768]{4,3,2,1,0:T(8,128)(2,1)S(1)}, bf16[1,1,16,16,768]{4,3,2,1,0:T(8,128)(2,1)}, u32[]{:S(2)}) copy-start(bf16[1,1,16,16,768]{4,3,2,1,0:T(8,128)(2,1)} %param.16) | copy-start | bytes 1179652
  3.6 34.4 %copy-start.5 = (bf16[1,1,16,16,768]{4,3,2,1,0:T(8,128)(2,1)S(1)}, bf16[1,1,16,16,768]{4,3,2,1,0:T(8,128)(2,1)}, u32[]{:S(2)}) copy-start(bf16[1,1,16,16,768]{4,3,2,1,0:T(8,128)(2,1)} %param.17) | copy-start | bytes 1179652
  5.3 32.8 %all-to-all-start = ((bf16[16,16,2048]{2,1,0:T(8,128)(2,1)}), bf16[16,16,2048]{2,1,0:T(8,128)(2,1)S(1)}, u32[]{:S(2)}, u32[]{:S(2)}) async-start(bf16[16,16,2048]{2,1,0:T(8,128)(2,1)} %bitcast.4), calls=%async_computation | async-start | bytes 2097152 | tf_op jit(solution)/shard_map/all_to_all | solution.py:182
  13.6 4.9 %collective-permute-start = (bf16[768,1024]{1,0:T(8,128)(2,1)S(1)}, bf16[768,1024]{1,0:T(8,128)(2,1)S(1)}, u32[]{:S(2)}, u32[]{:S(2)}) collective-permute-start(bf16[768,1024]{1,0:T(8,128)(2,1)S(1)} %bitcast.17), channel_id=1, source_target_pairs={{0,1},{1,0},{2,3},{3,2},{4,5},{5,4},{6,7},{7,6},{8,9},{9,8},{10,11... | collective-permute-start | bytes 4718600 | tf_op jit(solution)/shard_map/ppermute | solution.py:25
  13.7 27.1 %collective-permute-start.2 = (bf16[256,2048]{1,0:T(8,128)(2,1)}, bf16[256,2048]{1,0:T(8,128)(2,1)}, u32[]{:S(2)}, u32[]{:S(2)}) collective-permute-start(bf16[256,2048]{1,0:T(8,128)(2,1)} %bitcast.28), channel_id=1, source_target_pairs={{0,1},{1,0},{2,3},{3,2},{4,5},{5,4},{6,7},{7,6},{8,9},{9,8},{10,11... | collective-permute-start | bytes 3145736 | tf_op jit(solution)/shard_map/ppermute | solution.py:25
  18.5 1.1 copy-start.1
  38.0 1.4 copy-start.2
  39.4 1.4 copy-start.12
  40.7 2.4 %collective-permute-start.1 = (bf16[256,768]{1,0:T(8,128)(2,1)S(1)}, bf16[256,768]{1,0:T(8,128)(2,1)S(1)}, u32[]{:S(2)}, u32[]{:S(2)}) collective-permute-start(bf16[256,768]{1,0:T(8,128)(2,1)S(1)} %get-tuple-element.10), channel_id=1, source_target_pairs={{0,1},{1,0},{2,3},{3,2},{4,5},{5,4},{6,7},{7,6},{8,9},{9,8},{10,11... | collective-permute-start | bytes 1179656 | tf_op jit(solution)/shard_map/ppermute | solution.py:25
  43.2 9.4 %copy-start.10 = (bf16[1,1024,768]{2,1,0:T(8,128)(2,1)S(1)}, bf16[1,1024,768]{2,1,0:T(8,128)(2,1)}, u32[]{:S(2)}) copy-start(bf16[1,1024,768]{2,1,0:T(8,128)(2,1)} %param.19) | copy-start | bytes 4718596
  43.2 9.4 %copy-start.11 = (bf16[1,1024,768]{2,1,0:T(8,128)(2,1)S(1)}, bf16[1,1024,768]{2,1,0:T(8,128)(2,1)}, u32[]{:S(2)}) copy-start(bf16[1,1024,768]{2,1,0:T(8,128)(2,1)} %param.20) | copy-start | bytes 4718596
  50.1 2.5 %collective-permute-start.3 = (bf16[512,768]{1,0:T(8,128)(2,1)S(1)}, bf16[512,768]{1,0:T(8,128)(2,1)S(1)}, u32[]{:S(2)}, u32[]{:S(2)}) collective-permute-start(bf16[512,768]{1,0:T(8,128)(2,1)S(1)} %shard_map.125.own_ref), channel_id=1, source_target_pairs={{0,1},{1,0},{2,3},{3,2},{4,5},{5,4},{6,7},{7,6},{8,9},{9,8},{10,11... | collective-permute-start | bytes 2359304 | tf_op jit(solution)/shard_map/ppermute | solution.py:25
  54.6 43.5 %copy-start.3 = (bf16[1024,768]{1,0:T(8,128)(2,1)}, bf16[1024,768]{1,0:T(8,128)(2,1)S(1)}, u32[]{:S(2)}) copy-start(bf16[1024,768]{1,0:T(8,128)(2,1)S(1)} %get-tuple-element.14) | copy-start | bytes 4718596
  98.2 4.1 %copy-start.13 = (s32[16]{0:T(128)S(1)}, s32[16]{0:T(128)}, u32[]{:S(2)}) copy-start(s32[16]{0:T(128)} %param.21) | copy-start | bytes 196
  98.2 37.7 %all-to-all-start.1 = ((bf16[16,64,768]{2,1,0:T(8,128)(2,1)}), bf16[16,64,768]{2,1,0:T(8,128)(2,1)S(1)}, u32[]{:S(2)}, u32[]{:S(2)}) async-start(bf16[16,64,768]{2,1,0:T(8,128)(2,1)} %bitcast.19), calls=%async_computation.1 | async-start | bytes 3145728 | tf_op jit(solution)/shard_map/all_to_all | solution.py:182
  135.9 41.0 %all-to-all-start.4 = ((bf16[16,64,768]{2,1,0:T(8,128)(2,1)}), bf16[16,64,768]{2,1,0:T(8,128)(2,1)}, u32[]{:S(2)}, u32[]{:S(2)}) async-start(bf16[16,64,768]{2,1,0:T(8,128)(2,1)} %shard_map.128), calls=%async_computation.4 | async-start | bytes 3145728 | tf_op jit(solution)/shard_map/all_to_all | solution.py:182
  176.9 40.8 %all-to-all-start.2 = ((bf16[16,64,768]{2,1,0:T(8,128)(2,1)}), bf16[16,64,768]{2,1,0:T(8,128)(2,1)S(1)}, u32[]{:S(2)}, u32[]{:S(2)}) async-start(bf16[16,64,768]{2,1,0:T(8,128)(2,1)} %shard_map.127), calls=%async_computation.2 | async-start | bytes 3145728 | tf_op jit(solution)/shard_map/all_to_all | solution.py:182

commit v3 on v2

--- a/solution.py
+++ b/solution.py
@@ -140,25 +140,205 @@
             r_ref[...] = mixed.astype(jnp.bfloat16)
 
 
-def update_kernel(factor, rep_ref, own_ref, other_ref, xt_ref, gate_ref, up_ref, gate_out, up_out):
+def update_kernel(factor, halves, plane, rep_ref, me_ref, own_ref, other_ref, xt_ref, *refs):
+    weights, outs = refs[:2], refs[2:]
     rows = own_ref.shape[0] // 2
+    size = outs[0].shape[0]
     rep = rep_ref[0]
 
-    def update(weight_ref, out_ref, swapped):
+    def update(matrix, swapped):
         b_ref = other_ref if swapped else own_ref
-        first, second = (slice(rows, None), slice(0, rows)) if swapped else (slice(0, rows), slice(rows, None))
-        ortho = mm(xt_ref[:, :rows], b_ref[first]) + mm(xt_ref[:, rows:], b_ref[second])
-        out_ref[...] = (weight_ref[...].astype(jnp.float32) - factor * ortho).astype(jnp.bfloat16)
+        begin, end = slice(0, rows), slice(rows, None)
+        first, second = (end, begin) if swapped else (begin, end)
+        for h in range(halves):
+            for d in range(plane):
+                start = pl.multiple_of((h * plane + (me_ref[0] ^ d)) * size, size)
+                x = xt_ref[pl.ds(start, size), :]
+                ortho = mm(x[:, :rows], b_ref[first]) + mm(x[:, rows:], b_ref[second])
+                weight = weights[matrix][pl.ds(start, size), :].astype(jnp.float32)
+                outs[(matrix * halves + h) * plane + d][...] = (weight - factor * ortho).astype(
+                    jnp.bfloat16
+                )
 
     @pl.when(rep == 0)
     def _():
-        update(gate_ref, gate_out, False)
-        update(up_ref, up_out, True)
+        update(0, False)
+        update(1, True)
 
     @pl.when(rep == 1)
     def _():
-        update(gate_ref, gate_out, True)
-        update(up_ref, up_out, False)
+        update(0, True)
+        update(1, False)
+
+
+def route_kernel(line, plane, limit, owner_ref, place_ref, pick_ref, last_ref, count_ref, at, slot, right, left):
+    items = line * plane
+    mine, me = place_ref[0] // plane, place_ref[0] % plane
+
+    def begin(i, carry):
+        at[i] = i // plane
+        slot[i] = (i % plane) ^ me
+        return carry
+
+    lax.fori_loop(0, items, begin, 0)
+    count_ref[0] = 0
+    for step in range(limit):
+        for z in range(line):
+            right[z] = -1
+            left[z] = -1
+
+        def choose(i, carry):
+            place, target = at[i], owner_ref[i] // plane
+
+            @pl.when(target > place)
+            def _():
+                best = right[place]
+                reach = jnp.where(best >= 0, owner_ref[jnp.maximum(best, 0)] // plane, -1)
+                right[place] = jnp.where(target > reach, i, best)
+
+            @pl.when(target < place)
+            def _():
+                best = left[place]
+                reach = jnp.where(best >= 0, owner_ref[jnp.maximum(best, 0)] // plane, line)
+                left[place] = jnp.where(target < reach, i, best)
+
+            return carry + jnp.where(target != place, 1, 0)
+
+        waiting = lax.fori_loop(0, items, choose, jnp.int32(0))
+        count_ref[0] = jnp.where(waiting > 0, step + 1, count_ref[0])
+        go, back = right[mine], left[mine]
+        pick_ref[step] = jnp.where(go >= 0, slot[jnp.maximum(go, 0)], 0)
+        pick_ref[limit + step] = jnp.where(back >= 0, slot[jnp.maximum(back, 0)], 0)
+        for z in range(line):
+            for chosen, move in ((right, 1), (left, -1)):
+
+                @pl.when(chosen[z] >= 0)
+                def _():
+                    at[chosen[z]] = z + move
+                    slot[chosen[z]] = plane + step
+
+    def finish(i, carry):
+        target = owner_ref[i] // plane
+
+        @pl.when(target == mine)
+        def _():
+            late = (slot[i] >= plane) & (target < i // plane)
+            last_ref[(owner_ref[i] % plane) ^ me] = slot[i] + jnp.where(late, limit, 0)
+
+        return carry + jnp.where(target != at[i], 1, 0)
+
+    rest = lax.fori_loop(0, items, finish, jnp.int32(0))
+    count_ref[0] = jnp.where(rest > 0, limit + 1, count_ref[0])
+
+
+def route(line, plane, limit, owner, place):
+    table = lambda n: jax.ShapeDtypeStruct((n,), jnp.int32)
+    return pl.pallas_call(
+        functools.partial(route_kernel, line, plane, limit),
+        out_shape=(table(2 * limit), table(plane), table(1)),
+        in_specs=[SMEM, SMEM],
+        out_specs=(SMEM, SMEM, SMEM),
+        scratch_shapes=[pltpu.SMEM((n,), jnp.int32) for n in (line * plane, line * plane, line, line)],
+    )(owner, place)
+
+
+def pick_kernel(entries, groups, table_ref, *refs):
+    outs = refs[len(refs) - len(entries) :]
+    for entry, group, out in zip(entries, groups, outs):
+        for number, index in group:
+
+            @pl.when(table_ref[entry] == number)
+            def _():
+                out[...] = refs[index][...]
+
+
+def pick(table, blocks, entries, groups):
+    shape = jax.ShapeDtypeStruct(blocks[0].shape, blocks[0].dtype)
+    return call(
+        functools.partial(pick_kernel, entries, groups),
+        (shape,) * len(entries),
+        [SMEM] + [VMEM] * len(blocks),
+        (table, *blocks),
+        0,
+        4 * blocks[0].size * len(entries),
+        limit=16,
+    )
+
+
+def assemble_kernel(halves, plane, me_ref, *refs):
+    out_ref = refs[-1]
+    size = refs[0].shape[0]
+    for h in range(halves):
+        for d in range(plane):
+            start = pl.multiple_of((h * plane + (me_ref[0] ^ d)) * size, size)
+            out_ref[pl.ds(start, size), :] = refs[h * plane + d][...]
+
+
+def assemble(halves, plane, me, pieces):
+    rows, columns = pieces[0].shape
+    return call(
+        functools.partial(assemble_kernel, halves, plane),
+        jax.ShapeDtypeStruct((halves * plane * rows, columns), pieces[0].dtype),
+        [SMEM] + [VMEM] * len(pieces),
+        (me, *pieces),
+        0,
+        4 * halves * plane * rows * columns,
+        limit=16,
+    )
+
+
+def direct(steps, limit, line, plane, halves, me, pick_table, last_table, pieces):
+    items = line * plane
+
+    def across(block, d):
+        return lax.ppermute(block, "ep", [(i, i ^ d) for i in range(items)])
+
+    def along(block, move):
+        low, high = (0, items - plane) if move > 0 else (plane, items)
+        return lax.ppermute(block, "ep", [(i, i + move * plane) for i in range(low, high)])
+
+    chunks = [
+        [piece if d == 0 else across(piece, d) for d, piece in enumerate(pieces[c : c + plane])]
+        for c in range(0, len(pieces), plane)
+    ]
+    rights = [[] for _ in chunks]
+    lefts = [[] for _ in chunks]
+    base = [(s, s) for s in range(plane)]
+    for step in range(steps):
+        came = [(plane + s, plane + s) for s in range(step)]
+        back = [(plane + s, plane + step + s) for s in range(step)]
+        for c, chunk in enumerate(chunks):
+            go, ret = pick(
+                pick_table,
+                (*chunk, *rights[c], *lefts[c]),
+                (step, limit + step),
+                (base + came, base + back),
+            )
+            rights[c].append(along(go, 1))
+            lefts[c].append(along(ret, -1))
+    came = [(plane + s, plane + s) for s in range(steps)]
+    back = [(plane + limit + s, plane + steps + s) for s in range(steps)]
+    done = []
+    for c, chunk in enumerate(chunks):
+        found = pick(
+            last_table,
+            (*chunk, *rights[c], *lefts[c]),
+            tuple(range(plane)),
+            (base + came + back,) * plane,
+        )
+        done += [block if d == 0 else across(block, d) for d, block in enumerate(found)]
+    count = halves * plane
+    return tuple(assemble(halves, plane, me, done[m : m + count]) for m in (0, count))
+
+
+def indirect(experts, halves, plane, me, source, pieces):
+    count = halves * plane
+    results = []
+    for m in (0, count):
+        matrix = assemble(halves, plane, me, pieces[m : m + count])
+        results.append(exchange(matrix.reshape(experts, -1, matrix.shape[1])))
+    results = [exchange(arrange(spread, source)) for spread in results]
+    return tuple(result.reshape(-1, result.shape[2]) for result in results)
 
 
 def arrange_kernel(index_ref, in_ref, out_ref):
@@ -251,25 +431,47 @@
         ),
     )
     other_b = from_partner(own_b)
-    gate, up = call(
-        functools.partial(update_kernel, step_scale * math.sqrt(width)),
-        (shape(half, inner), shape(half, inner)),
-        [SMEM] + [VMEM] * 5,
-        (rep, own_b, other_b, transposed, gate_weight[0], up_weight[0]),
+    halves = 2
+    plane = 1
+    while 4 * plane * plane <= experts:
+        plane *= 2
+    line = experts // plane
+    place = lax.axis_index("ep").astype(jnp.int32).reshape(1)
+    me = place % plane
+    order = jnp.arange(experts, dtype=jnp.int32)
+    source = jnp.sum(
+        jnp.where(new_owner[None, :] == order[:, None], order[None, :], 0), axis=1, dtype=jnp.int32
+    )
+    pieces = call(
+        functools.partial(update_kernel, step_scale * math.sqrt(width), halves, plane),
+        (shape(half // (halves * plane), inner),) * (2 * halves * plane),
+        [SMEM, SMEM] + [VMEM] * 5,
+        (rep, me, own_b, other_b, transposed, gate_weight[0], up_weight[0]),
         2 * 2 * half * 2 * rows * inner,
         8 * half * inner,
     )
-    place = jnp.arange(experts, dtype=jnp.int32)
-    source = jnp.sum(
-        jnp.where(new_owner[None, :] == place[:, None], place[None, :], 0), axis=1, dtype=jnp.int32
-    )
-    pieces = (experts, half // experts, inner)
-    results = []
-    for matrix in (gate, up):
-        spread = exchange(matrix.reshape(pieces))
-        results.append(spread)
-    results = [exchange(arrange(spread, source)).reshape(1, half, inner) for spread in results]
-    return tuple(results)
+    if line == plane:
+        least, limit = plane - 1, plane + 2
+        pick_table, last_table, count = route(line, plane, limit, new_owner, place)
+        branches = [
+            functools.partial(direct, steps, limit, line, plane, halves)
+            for steps in range(least, limit + 1)
+        ]
+
+        def other(me, pick_table, last_table, pieces):
+            return indirect(experts, halves, plane, me, source, pieces)
+
+        gate, up = lax.switch(
+            jnp.maximum(count[0] - least, 0),
+            branches + [other],
+            me,
+            pick_table,
+            last_table,
+            pieces,
+        )
+    else:
+        gate, up = indirect(experts, halves, plane, me, source, pieces)
+    return (gate[None], up[None])
 
 
 def solution(mesh):

time: 224 us -> 252 us (1.12); the launches traced: 222 us -> 255 us
  starting transfers between devices: 28.2 us -> 133 us
  waiting for transfers between devices: 122 us -> 50 us
  blocking collectives: 43.5 us -> 0 us
  Pallas kernels: 17.8 us -> 37.7 us
  loops' own time: 0 us -> 19.2 us
  local copies, waits for them, and re-layouts: 9.34 us -> 12.7 us
    ppermute x0 -> x56, starting transfers between devices: none -> 124 us  [the longest x32 93.4 us: along(): lax.ppermute(block, 'ep', [(i, i + move * plane) for i in range(low, high)])]
    all_to_all x4 -> x1, waiting for transfers between devices: 116 us -> 18.4 us  [exchange(): return lax.all_to_all(blocks, 'ep', split_axis=0, concat_axis=0, tiled=True)]
    all_to_all x1 -> x0, blocking collectives: 43.5 us -> none  [exchange(): return lax.all_to_all(blocks, 'ep', split_axis=0, concat_axis=0, tiled=True)]
    ppermute x0 -> x56, waiting for transfers between devices: none -> 27.3 us  [the longest x24 27.2 us: across(): return lax.ppermute(block, 'ep', [(i, i ^ d) for i in range(items)])]
    another operation x0 -> x1, loops' own time: none -> 19.2 us  [shards(): lax.switch(jnp.maximum(count[0] - least, 0), branches + [other], me, pick...]
    all_to_all x4 -> x1, starting transfers between devices: 27 us -> 8.31 us  [exchange(): return lax.all_to_all(blocks, 'ep', split_axis=0, concat_axis=0, tiled=True)]
    pallas_call x6 -> x26, Pallas kernels: 16.1 us -> 30.4 us  [call(): pl.pallas_call(kernel, out_shape=outs, in_specs=in_specs, out_specs=jax.t...]
    pallas_call x0 -> x1, Pallas kernels: none -> 5.67 us  [route(): pl.pallas_call(functools.partial(route_kernel, line, plane, limit), out_s...]
  transfers between devices with their start and end apart: 8 -> 61, of which waited for: 6 -> 16; matrix products, arithmetic and copies ran while one was open for 0% -> 0% of each run, Pallas kernels for 3% -> 9%
where the time goes in v3:
time: 252 us; the launch traced here: 255 us
  starting transfers between devices  133 us (53%)
  waiting for transfers between devices  50 us (20%)
  Pallas kernels  37.7 us (15%)
  loops' own time  19.2 us (8%)
  local copies, waits for them, and re-layouts  12.7 us (5%)
    ppermute x32, starting transfers between devices, along(): lax.ppermute(block, 'ep', [(i, i + move * plane) for i in range(low, high)])  93.4 us
    pallas_call x26, Pallas kernels, call(): pl.pallas_call(kernel, out_shape=outs, in_specs=in_specs, out_specs=jax.t...  30.4 us
    ppermute x24, starting transfers between devices, across(): return lax.ppermute(block, 'ep', [(i, i ^ d) for i in range(items)])  30.4 us
    ppermute x24, waiting for transfers between devices, across(): return lax.ppermute(block, 'ep', [(i, i ^ d) for i in range(items)])  27.2 us
    another operation x1, loops' own time, shards(): lax.switch(jnp.maximum(count[0] - least, 0), branches + [other], me, pick...  19.2 us
    all_to_all x1, waiting for transfers between devices, exchange(): return lax.all_to_all(blocks, 'ep', split_axis=0, concat_axis=0, tiled=True)  18.4 us
    unnamed x32, local copies, waits for them, and re-layouts  11.5 us
    all_to_all x1, starting transfers between devices, exchange(): return lax.all_to_all(blocks, 'ep', split_axis=0, concat_axis=0, tiled=True)  8.31 us
  transfers between devices with their start and end apart: 61, of which 16 were waited for; matrix products, arithmetic and copies ran while one was open for 0% of the time, Pallas kernels for 9%

profile of v3, /device:TPU:0, one launch (start us, length us, event | category | flops | bytes accessed | tf_op | source)
XLA Modules:
  0.0 254.7 jit_solution(2693548207009467107)
XLA Ops:
  3.6 1.6 shard_map.133
  5.3 8.3 %all-to-all-start.4 = ((bf16[16,16,2048]{2,1,0:T(8,128)(2,1)}), bf16[16,16,2048]{2,1,0:T(8,128)(2,1)S(1)}, u32[]{:S(2)}, u32[]{:S(2)}) async-start(bf16[16,16,2048]{2,1,0:T(8,128)(2,1)} %bitcast.18), calls=%async_computation.4 | async-start | bytes 2097152 | tf_op jit(solution)/shard_map/all_to_all | solution.py:362
  14.2 4.4 %collective-permute-done.240.other_down_ref = bf16[768,1024]{1,0:T(8,128)(2,1)S(1)} collective-permute-done((bf16[768,1024]{1,0:T(8,128)(2,1)S(1)}, bf16[768,1024]{1,0:T(8,128)(2,1)S(1)}, u32[]{:S(2)}, u32[]{:S(2)}) %collective-permute-start.240) | collective-permute-done | bytes 1572896 | tf_op jit(solution)/shard_map/ppermute | solution.py:25
  19.7 18.4 %all-to-all-done.4 = bf16[16,16,2048]{2,1,0:T(8,128)(2,1)S(1)} async-done(((bf16[16,16,2048]{2,1,0:T(8,128)(2,1)}), bf16[16,16,2048]{2,1,0:T(8,128)(2,1)S(1)}, u32[]{:S(2)}, u32[]{:S(2)}) %all-to-all-start.4) | async-done | bytes 1048608 | tf_op jit(solution)/shard_map/all_to_all | solution.py:362
  38.0 1.4 copy-done.4
  40.8 2.3 shard_map.135
  44.1 7.8 %shard_map.136.own_ref = bf16[512,768]{1,0:T(8,128)(2,1)} custom-call(bf16[256,768]{1,0:T(8,128)(2,1)S(1)} %get-tuple-element.532.own_ref, bf16[256,768]{1,0:T(8,128)(2,1)S(1)} %collective-permute-done.241.other_ref, bf16[512,512]{1,0:T(8,128)(2,1)S(1)} %get-tuple-element.534.high_ref, bf16[512,512]{1,0:T(8,128)(2,1)S(1)} %get-tuple-element.535.low_ref), custom_call_target="tpu_custom_call" | custom-call | flops 5435817984 | bytes 1572864 | tf_op jit(solution)/shard_map/pallas_call | solution.py:33
  52.4 5.7 %shard_map.132 = (s32[12]{0:T(128)S(1)}, s32[4]{0:T(128)S(1)}, s32[1]{0:T(128)}) custom-call(s32[16]{0:T(128)S(1)} %copy-done.34, s32[1]{0:T(128)} %bitcast.12.place_ref), custom_call_target="tpu_custom_call" | custom-call | tf_op jit(solution)/shard_map/pallas_call | solution.py:236
  60.0 3.5 %shard_map.137 = (bf16[128,768]{1,0:T(8,128)(2,1)S(1)}, bf16[128,768]{1,0:T(8,128)(2,1)S(1)}, bf16[128,768]{1,0:T(8,128)(2,1)S(1)}, bf16[128,768]{1,0:T(8,128)(2...) custom-call(s32[1]{0:T(128)} %bitcast.14.rep_ref, ...), custom_call_target="tpu_custom_call" | custom-call | flops 1610612736 | bytes 6291456 | tf_op jit(solution)/shard_map/pallas_call | solution.py:33
  64.6 185.8 %conditional.1 = (bf16[1,1024,768]{2,1,0:T(8,128)(2,1)}, bf16[1,1024,768]{2,1,0:T(8,128)(2,1)S(1)}) conditional(s32[]{:T(128)} %bitcast.13, (bf16[128,768]{1,0:T(8,128)(2,1)S(1)}, bf16[128,768]{1,0:T(8,128)(2,1)S(1)}, bf16[128,768]{1,0:T(8,128)(2,1)S(1)}, s32[12]{0:T(128)S(1)}, bf16[128,768]{1,0:T(8,128)(2,1)S(1)}, ...), branch_computations={%region_0.1_spmd, %region_1.2_spmd, %region_2.3_spmd, %region_3.4_... | conditional | flops 752 | bytes 88083280 | solution.py:464
  65.2 2.0 collective-permute-start.49
  67.2 1.5 collective-permute-start.62
  69.3 3.2 %collective-permute-done.48.refs_1_ = bf16[128,768]{1,0:T(8,128)(2,1)S(1)} collective-permute-done((bf16[128,768]{1,0:T(8,128)(2,1)S(1)}, bf16[128,768]{1,0:T(8,128)(2,1)S(1)}, u32[]{:S(2)}, u32[]{:S(2)}) %collective-permute-start.48) | collective-permute-done | bytes 196640 | tf_op jit(solution)/shard_map/cond/branch_1_fun/ppermute | solution.py:294
  72.4 2.0 collective-permute-start.92
  74.4 1.5 collective-permute-start.76
  76.6 2.0 collective-permute-start.77
  78.6 2.2 collective-permute-done.90.refs_1_
  80.8 2.0 collective-permute-start.78
  82.9 3.6 %collective-permute-done.92.refs_3_ = bf16[128,768]{1,0:T(8,128)(2,1)S(1)} collective-permute-done((bf16[128,768]{1,0:T(8,128)(2,1)S(1)}, bf16[128,768]{1,0:T(8,128)(2,1)S(1)}, u32[]{:S(2)}, u32[]{:S(2)}) %collective-permute-start.92) | collective-permute-done | bytes 196640 | tf_op jit(solution)/shard_map/cond/branch_1_fun/ppermute | solution.py:294
  87.2 2.1 collective-permute-done.76.refs_1_
  89.3 2.0 collective-permute-start.50
  91.3 4.2 %collective-permute-start.93 = (bf16[128,768]{1,0:T(8,128)(2,1)S(1)}, bf16[128,768]{1,0:T(8,128)(2,1)S(1)}, u32[]{:S(2)}, u32[]{:S(2)}) collective-permute-start(bf16[128,768]{1,0:T(8,128)(2,1)S(1)} %get-tuple-element.315), channel_id=1, source_target_pairs={{0,8},{2,10},{4,12},{6,14},{8,16},{10,18},{12,20},{14,22},{16,24},... | collective-permute-start | bytes 589832 | tf_op jit(solution)/shard_map/cond/branch_1_fun/ppermute | solution.py:298
  97.5 5.9 %collective-permute-done.63.refs_2_ = bf16[128,768]{1,0:T(8,128)(2,1)S(1)} collective-permute-done((bf16[128,768]{1,0:T(8,128)(2,1)S(1)}, bf16[128,768]{1,0:T(8,128)(2,1)S(1)}, u32[]{:S(2)}, u32[]{:S(2)}) %collective-permute-start.63) | collective-permute-done | bytes 196640 | tf_op jit(solution)/shard_map/cond/branch_1_fun/ppermute | solution.py:294
  103.4 4.6 %collective-permute-start.79 = (bf16[128,768]{1,0:T(8,128)(2,1)S(1)}, bf16[128,768]{1,0:T(8,128)(2,1)S(1)}, u32[]{:S(2)}, u32[]{:S(2)}) collective-permute-start(bf16[128,768]{1,0:T(8,128)(2,1)S(1)} %get-tuple-element.299), channel_id=1, source_target_pairs={{0,8},{2,10},{4,12},{6,14},{8,16},{10,18},{12,20},{14,22},{16,24},... | collective-permute-start | bytes 589832 | tf_op jit(solution)/shard_map/cond/branch_1_fun/ppermute | solution.py:298
  110.0 4.6 %collective-permute-start.65 = (bf16[128,768]{1,0:T(8,128)(2,1)S(1)}, bf16[128,768]{1,0:T(8,128)(2,1)S(1)}, u32[]{:S(2)}, u32[]{:S(2)}) collective-permute-start(bf16[128,768]{1,0:T(8,128)(2,1)S(1)} %get-tuple-element.283), channel_id=1, source_target_pairs={{0,8},{2,10},{4,12},{6,14},{8,16},{10,18},{12,20},{14,22},{16,24},... | collective-permute-start | bytes 589832 | tf_op jit(solution)/shard_map/cond/branch_1_fun/ppermute | solution.py:298
  116.5 4.6 %collective-permute-start.51 = (bf16[128,768]{1,0:T(8,128)(2,1)S(1)}, bf16[128,768]{1,0:T(8,128)(2,1)S(1)}, u32[]{:S(2)}, u32[]{:S(2)}) collective-permute-start(bf16[128,768]{1,0:T(8,128)(2,1)S(1)} %get-tuple-element.267), channel_id=1, source_target_pairs={{0,8},{2,10},{4,12},{6,14},{8,16},{10,18},{12,20},{14,22},{16,24},... | collective-permute-start | bytes 589832 | tf_op jit(solution)/shard_map/cond/branch_1_fun/ppermute | solution.py:298
  123.0 4.6 %collective-permute-start.95 = (bf16[128,768]{1,0:T(8,128)(2,1)S(1)}, bf16[128,768]{1,0:T(8,128)(2,1)S(1)}, u32[]{:S(2)}, u32[]{:S(2)}) collective-permute-start(bf16[128,768]{1,0:T(8,128)(2,1)S(1)} %get-tuple-element.317), channel_id=1, source_target_pairs={{0,8},{2,10},{4,12},{6,14},{8,16},{10,18},{12,20},{14,22},{16,24},... | collective-permute-start | bytes 589832 | tf_op jit(solution)/shard_map/cond/branch_1_fun/ppermute | solution.py:298
  129.6 4.6 %collective-permute-start.81 = (bf16[128,768]{1,0:T(8,128)(2,1)S(1)}, bf16[128,768]{1,0:T(8,128)(2,1)S(1)}, u32[]{:S(2)}, u32[]{:S(2)}) collective-permute-start(bf16[128,768]{1,0:T(8,128)(2,1)S(1)} %get-tuple-element.301), channel_id=1, source_target_pairs={{0,8},{2,10},{4,12},{6,14},{8,16},{10,18},{12,20},{14,22},{16,24},... | collective-permute-start | bytes 589832 | tf_op jit(solution)/shard_map/cond/branch_1_fun/ppermute | solution.py:298
  136.1 4.6 %collective-permute-start.67 = (bf16[128,768]{1,0:T(8,128)(2,1)S(1)}, bf16[128,768]{1,0:T(8,128)(2,1)S(1)}, u32[]{:S(2)}, u32[]{:S(2)}) collective-permute-start(bf16[128,768]{1,0:T(8,128)(2,1)S(1)} %get-tuple-element.285), channel_id=1, source_target_pairs={{0,8},{2,10},{4,12},{6,14},{8,16},{10,18},{12,20},{14,22},{16,24},... | collective-permute-start | bytes 589832 | tf_op jit(solution)/shard_map/cond/branch_1_fun/ppermute | solution.py:298
  142.6 4.6 %collective-permute-start.53 = (bf16[128,768]{1,0:T(8,128)(2,1)S(1)}, bf16[128,768]{1,0:T(8,128)(2,1)S(1)}, u32[]{:S(2)}, u32[]{:S(2)}) collective-permute-start(bf16[128,768]{1,0:T(8,128)(2,1)S(1)} %get-tuple-element.269), channel_id=1, source_target_pairs={{0,8},{2,10},{4,12},{6,14},{8,16},{10,18},{12,20},{14,22},{16,24},... | collective-permute-start | bytes 589832 | tf_op jit(solution)/shard_map/cond/branch_1_fun/ppermute | solution.py:298
  147.2 1.3 collective-permute-start.54
  149.2 4.6 %collective-permute-start.97 = (bf16[128,768]{1,0:T(8,128)(2,1)S(1)}, bf16[128,768]{1,0:T(8,128)(2,1)S(1)}, u32[]{:S(2)}, u32[]{:S(2)}) collective-permute-start(bf16[128,768]{1,0:T(8,128)(2,1)S(1)} %get-tuple-element.319), channel_id=1, source_target_pairs={{0,8},{2,10},{4,12},{6,14},{8,16},{10,18},{12,20},{14,22},{16,24},... | collective-permute-start | bytes 589832 | tf_op jit(solution)/shard_map/cond/branch_1_fun/ppermute | solution.py:298
  155.7 4.6 %collective-permute-start.83 = (bf16[128,768]{1,0:T(8,128)(2,1)S(1)}, bf16[128,768]{1,0:T(8,128)(2,1)S(1)}, u32[]{:S(2)}, u32[]{:S(2)}) collective-permute-start(bf16[128,768]{1,0:T(8,128)(2,1)S(1)} %get-tuple-element.303), channel_id=1, source_target_pairs={{0,8},{2,10},{4,12},{6,14},{8,16},{10,18},{12,20},{14,22},{16,24},... | collective-permute-start | bytes 589832 | tf_op jit(solution)/shard_map/cond/branch_1_fun/ppermute | solution.py:298
  162.3 4.6 %collective-permute-start.69 = (bf16[128,768]{1,0:T(8,128)(2,1)S(1)}, bf16[128,768]{1,0:T(8,128)(2,1)S(1)}, u32[]{:S(2)}, u32[]{:S(2)}) collective-permute-start(bf16[128,768]{1,0:T(8,128)(2,1)S(1)} %get-tuple-element.287), channel_id=1, source_target_pairs={{0,8},{2,10},{4,12},{6,14},{8,16},{10,18},{12,20},{14,22},{16,24},... | collective-permute-start | bytes 589832 | tf_op jit(solution)/shard_map/cond/branch_1_fun/ppermute | solution.py:298
  168.8 4.6 %collective-permute-start.55 = (bf16[128,768]{1,0:T(8,128)(2,1)S(1)}, bf16[128,768]{1,0:T(8,128)(2,1)S(1)}, u32[]{:S(2)}, u32[]{:S(2)}) collective-permute-start(bf16[128,768]{1,0:T(8,128)(2,1)S(1)} %get-tuple-element.271), channel_id=1, source_target_pairs={{0,8},{2,10},{4,12},{6,14},{8,16},{10,18},{12,20},{14,22},{16,24},... | collective-permute-start | bytes 589832 | tf_op jit(solution)/shard_map/cond/branch_1_fun/ppermute | solution.py:298
  173.4 1.3 collective-permute-start.56
  175.4 4.6 %collective-permute-start.99 = (bf16[128,768]{1,0:T(8,128)(2,1)S(1)}, bf16[128,768]{1,0:T(8,128)(2,1)S(1)}, u32[]{:S(2)}, u32[]{:S(2)}) collective-permute-start(bf16[128,768]{1,0:T(8,128)(2,1)S(1)} %get-tuple-element.321), channel_id=1, source_target_pairs={{0,8},{2,10},{4,12},{6,14},{8,16},{10,18},{12,20},{14,22},{16,24},... | collective-permute-start | bytes 589832 | tf_op jit(solution)/shard_map/cond/branch_1_fun/ppermute | solution.py:298
  182.0 4.6 %collective-permute-start.85 = (bf16[128,768]{1,0:T(8,128)(2,1)S(1)}, bf16[128,768]{1,0:T(8,128)(2,1)S(1)}, u32[]{:S(2)}, u32[]{:S(2)}) collective-permute-start(bf16[128,768]{1,0:T(8,128)(2,1)S(1)} %get-tuple-element.305), channel_id=1, source_target_pairs={{0,8},{2,10},{4,12},{6,14},{8,16},{10,18},{12,20},{14,22},{16,24},... | collective-permute-start | bytes 589832 | tf_op jit(solution)/shard_map/cond/branch_1_fun/ppermute | solution.py:298
  188.5 4.6 %collective-permute-start.71 = (bf16[128,768]{1,0:T(8,128)(2,1)S(1)}, bf16[128,768]{1,0:T(8,128)(2,1)S(1)}, u32[]{:S(2)}, u32[]{:S(2)}) collective-permute-start(bf16[128,768]{1,0:T(8,128)(2,1)S(1)} %get-tuple-element.289), channel_id=1, source_target_pairs={{0,8},{2,10},{4,12},{6,14},{8,16},{10,18},{12,20},{14,22},{16,24},... | collective-permute-start | bytes 589832 | tf_op jit(solution)/shard_map/cond/branch_1_fun/ppermute | solution.py:298
  195.1 4.6 %collective-permute-start.57 = (bf16[128,768]{1,0:T(8,128)(2,1)S(1)}, bf16[128,768]{1,0:T(8,128)(2,1)S(1)}, u32[]{:S(2)}, u32[]{:S(2)}) collective-permute-start(bf16[128,768]{1,0:T(8,128)(2,1)S(1)} %get-tuple-element.273), channel_id=1, source_target_pairs={{0,8},{2,10},{4,12},{6,14},{8,16},{10,18},{12,20},{14,22},{16,24},... | collective-permute-start | bytes 589832 | tf_op jit(solution)/shard_map/cond/branch_1_fun/ppermute | solution.py:298
  204.6 2.0 collective-permute-start.103
  211.1 2.5 collective-permute-done.102.refs_6_
  213.6 2.3 collective-permute-start.73
  219.4 3.5 %collective-permute-start.59 = (bf16[128,768]{1,0:T(8,128)(2,1)S(1)}, bf16[128,768]{1,0:T(8,128)(2,1)S(1)}, u32[]{:S(2)}, u32[]{:S(2)}) collective-permute-start(bf16[128,768]{1,0:T(8,128)(2,1)S(1)} %get-tuple-element.276), channel_id=1, source_target_pairs={{0,2},{2,0},{4,6},{6,4},{8,10},{10,8},{12,14},{14,12},{16,18},{18,... | collective-permute-start | bytes 589832 | tf_op jit(solution)/shard_map/cond/branch_1_fun/ppermute | solution.py:294
  223.3 1.6 collective-permute-start.61
  225.7 1.8 collective-permute-done.59.refs_1_
  227.5 3.2 %collective-permute-done.60.refs_2_ = bf16[128,768]{1,0:T(8,128)(2,1)S(1)} collective-permute-done((bf16[128,768]{1,0:T(8,128)(2,1)S(1)}, bf16[128,768]{1,0:T(8,128)(2,1)S(1)}, u32[]{:S(2)}, u32[]{:S(2)}) %collective-permute-start.60) | collective-permute-done | bytes 196640 | tf_op jit(solution)/shard_map/cond/branch_1_fun/ppermute | solution.py:294
  250.4 2.7 %copy.35 = bf16[1,1024,768]{2,1,0:T(8,128)(2,1)} copy(bf16[1,1024,768]{2,1,0:T(8,128)(2,1)} %get-tuple-element.569) | data formatting | bytes 3145728
  (137 shorter events, 55.5 us)
Async XLA Ops:
  5.3 32.8 %all-to-all-start.4 = ((bf16[16,16,2048]{2,1,0:T(8,128)(2,1)}), bf16[16,16,2048]{2,1,0:T(8,128)(2,1)S(1)}, u32[]{:S(2)}, u32[]{:S(2)}) async-start(bf16[16,16,2048]{2,1,0:T(8,128)(2,1)} %bitcast.18), calls=%async_computation.4 | async-start | bytes 2097152 | tf_op jit(solution)/shard_map/all_to_all | solution.py:362
  13.7 27.1 %collective-permute-start.242 = (bf16[256,2048]{1,0:T(8,128)(2,1)}, bf16[256,2048]{1,0:T(8,128)(2,1)}, u32[]{:S(2)}, u32[]{:S(2)}) collective-permute-start(bf16[256,2048]{1,0:T(8,128)(2,1)} %bitcast.37), channel_id=1, source_target_pairs={{0,1},{1,0},{2,3},{3,2},{4,5},{5,4},{6,7},{7,6},{8,9},{9,8},{10,11... | collective-permute-start | bytes 3145736 | tf_op jit(solution)/shard_map/ppermute | solution.py:25
  68.7 12.2 %collective-permute-start.90 = (bf16[128,768]{1,0:T(8,128)(2,1)S(1)}, bf16[128,768]{1,0:T(8,128)(2,1)S(1)}, u32[]{:S(2)}, u32[]{:S(2)}) collective-permute-start(bf16[128,768]{1,0:T(8,128)(2,1)S(1)} %get-tuple-element.312), channel_id=1, source_target_pairs={{0,2},{2,0},{4,6},{6,4},{8,10},{10,8},{12,14},{14,12},{16,18},{18,... | collective-permute-start | bytes 589832 | tf_op jit(solution)/shard_map/cond/branch_1_fun/ppermute | solution.py:294
  69.2 13.6 %collective-permute-start.91 = (bf16[128,768]{1,0:T(8,128)(2,1)S(1)}, bf16[128,768]{1,0:T(8,128)(2,1)S(1)}, u32[]{:S(2)}, u32[]{:S(2)}) collective-permute-start(bf16[128,768]{1,0:T(8,128)(2,1)S(1)} %get-tuple-element.313), channel_id=1, source_target_pairs={{0,4},{2,6},{4,0},{6,2},{8,12},{10,14},{12,8},{14,10},{16,20},{18,... | collective-permute-start | bytes 589832 | tf_op jit(solution)/shard_map/cond/branch_1_fun/ppermute | solution.py:294
  72.4 14.1 %collective-permute-start.92 = (bf16[128,768]{1,0:T(8,128)(2,1)S(1)}, bf16[128,768]{1,0:T(8,128)(2,1)S(1)}, u32[]{:S(2)}, u32[]{:S(2)}) collective-permute-start(bf16[128,768]{1,0:T(8,128)(2,1)S(1)} %get-tuple-element.314), channel_id=1, source_target_pairs={{0,6},{2,4},{4,2},{6,0},{8,14},{10,12},{12,10},{14,8},{16,22},{18,... | collective-permute-start | bytes 589832 | tf_op jit(solution)/shard_map/cond/branch_1_fun/ppermute | solution.py:294
  74.4 14.9 %collective-permute-start.76 = (bf16[128,768]{1,0:T(8,128)(2,1)S(1)}, bf16[128,768]{1,0:T(8,128)(2,1)S(1)}, u32[]{:S(2)}, u32[]{:S(2)}) collective-permute-start(bf16[128,768]{1,0:T(8,128)(2,1)S(1)} %get-tuple-element.296), channel_id=1, source_target_pairs={{0,2},{2,0},{4,6},{6,4},{8,10},{10,8},{12,14},{14,12},{16,18},{18,... | collective-permute-start | bytes 589832 | tf_op jit(solution)/shard_map/cond/branch_1_fun/ppermute | solution.py:294
  76.6 14.7 %collective-permute-start.77 = (bf16[128,768]{1,0:T(8,128)(2,1)S(1)}, bf16[128,768]{1,0:T(8,128)(2,1)S(1)}, u32[]{:S(2)}, u32[]{:S(2)}) collective-permute-start(bf16[128,768]{1,0:T(8,128)(2,1)S(1)} %get-tuple-element.297), channel_id=1, source_target_pairs={{0,4},{2,6},{4,0},{6,2},{8,12},{10,14},{12,8},{14,10},{16,20},{18,... | collective-permute-start | bytes 589832 | tf_op jit(solution)/shard_map/cond/branch_1_fun/ppermute | solution.py:294
  80.8 14.7 %collective-permute-start.78 = (bf16[128,768]{1,0:T(8,128)(2,1)S(1)}, bf16[128,768]{1,0:T(8,128)(2,1)S(1)}, u32[]{:S(2)}, u32[]{:S(2)}) collective-permute-start(bf16[128,768]{1,0:T(8,128)(2,1)S(1)} %get-tuple-element.298), channel_id=1, source_target_pairs={{0,6},{2,4},{4,2},{6,0},{8,14},{10,12},{12,10},{14,8},{16,22},{18,... | collective-permute-start | bytes 589832 | tf_op jit(solution)/shard_map/cond/branch_1_fun/ppermute | solution.py:294
  82.8 20.5 %collective-permute-start.63 = (bf16[128,768]{1,0:T(8,128)(2,1)S(1)}, bf16[128,768]{1,0:T(8,128)(2,1)S(1)}, u32[]{:S(2)}, u32[]{:S(2)}) collective-permute-start(bf16[128,768]{1,0:T(8,128)(2,1)S(1)} %get-tuple-element.281), channel_id=1, source_target_pairs={{0,4},{2,6},{4,0},{6,2},{8,12},{10,14},{12,8},{14,10},{16,20},{18,... | collective-permute-start | bytes 589832 | tf_op jit(solution)/shard_map/cond/branch_1_fun/ppermute | solution.py:294
  86.5 21.5 %collective-permute-start.64 = (bf16[128,768]{1,0:T(8,128)(2,1)S(1)}, bf16[128,768]{1,0:T(8,128)(2,1)S(1)}, u32[]{:S(2)}, u32[]{:S(2)}) collective-permute-start(bf16[128,768]{1,0:T(8,128)(2,1)S(1)} %get-tuple-element.282), channel_id=1, source_target_pairs={{0,6},{2,4},{4,2},{6,0},{8,14},{10,12},{12,10},{14,8},{16,22},{18,... | collective-permute-start | bytes 589832 | tf_op jit(solution)/shard_map/cond/branch_1_fun/ppermute | solution.py:294
  89.3 20.6 %collective-permute-start.50 = (bf16[128,768]{1,0:T(8,128)(2,1)S(1)}, bf16[128,768]{1,0:T(8,128)(2,1)S(1)}, u32[]{:S(2)}, u32[]{:S(2)}) collective-permute-start(bf16[128,768]{1,0:T(8,128)(2,1)S(1)} %get-tuple-element.265), channel_id=1, source_target_pairs={{0,6},{2,4},{4,2},{6,0},{8,14},{10,12},{12,10},{14,8},{16,22},{18,... | collective-permute-start | bytes 589832 | tf_op jit(solution)/shard_map/cond/branch_1_fun/ppermute | solution.py:294
  91.3 23.2 %collective-permute-start.93 = (bf16[128,768]{1,0:T(8,128)(2,1)S(1)}, bf16[128,768]{1,0:T(8,128)(2,1)S(1)}, u32[]{:S(2)}, u32[]{:S(2)}) collective-permute-start(bf16[128,768]{1,0:T(8,128)(2,1)S(1)} %get-tuple-element.315), channel_id=1, source_target_pairs={{0,8},{2,10},{4,12},{6,14},{8,16},{10,18},{12,20},{14,22},{16,24},... | collective-permute-start | bytes 589832 | tf_op jit(solution)/shard_map/cond/branch_1_fun/ppermute | solution.py:298
  95.5 20.9 %collective-permute-start.94 = (bf16[128,768]{1,0:T(8,128)(2,1)S(1)}, bf16[128,768]{1,0:T(8,128)(2,1)S(1)}, u32[]{:S(2)}, u32[]{:S(2)}) collective-permute-start(bf16[128,768]{1,0:T(8,128)(2,1)S(1)} %get-tuple-element.316), channel_id=1, source_target_pairs={{8,0},{10,2},{12,4},{14,6},{16,8},{18,10},{20,12},{22,14},{24,16},... | collective-permute-start | bytes 589832 | tf_op jit(solution)/shard_map/cond/branch_1_fun/ppermute | solution.py:298
  103.4 18.3 %collective-permute-start.79 = (bf16[128,768]{1,0:T(8,128)(2,1)S(1)}, bf16[128,768]{1,0:T(8,128)(2,1)S(1)}, u32[]{:S(2)}, u32[]{:S(2)}) collective-permute-start(bf16[128,768]{1,0:T(8,128)(2,1)S(1)} %get-tuple-element.299), channel_id=1, source_target_pairs={{0,8},{2,10},{4,12},{6,14},{8,16},{10,18},{12,20},{14,22},{16,24},... | collective-permute-start | bytes 589832 | tf_op jit(solution)/shard_map/cond/branch_1_fun/ppermute | solution.py:298
  108.0 15.0 %collective-permute-start.80 = (bf16[128,768]{1,0:T(8,128)(2,1)S(1)}, bf16[128,768]{1,0:T(8,128)(2,1)S(1)}, u32[]{:S(2)}, u32[]{:S(2)}) collective-permute-start(bf16[128,768]{1,0:T(8,128)(2,1)S(1)} %get-tuple-element.300), channel_id=1, source_target_pairs={{8,0},{10,2},{12,4},{14,6},{16,8},{18,10},{20,12},{22,14},{24,16},... | collective-permute-start | bytes 589832 | tf_op jit(solution)/shard_map/cond/branch_1_fun/ppermute | solution.py:298
  110.0 18.3 %collective-permute-start.65 = (bf16[128,768]{1,0:T(8,128)(2,1)S(1)}, bf16[128,768]{1,0:T(8,128)(2,1)S(1)}, u32[]{:S(2)}, u32[]{:S(2)}) collective-permute-start(bf16[128,768]{1,0:T(8,128)(2,1)S(1)} %get-tuple-element.283), channel_id=1, source_target_pairs={{0,8},{2,10},{4,12},{6,14},{8,16},{10,18},{12,20},{14,22},{16,24},... | collective-permute-start | bytes 589832 | tf_op jit(solution)/shard_map/cond/branch_1_fun/ppermute | solution.py:298
  114.5 15.0 %collective-permute-start.66 = (bf16[128,768]{1,0:T(8,128)(2,1)S(1)}, bf16[128,768]{1,0:T(8,128)(2,1)S(1)}, u32[]{:S(2)}, u32[]{:S(2)}) collective-permute-start(bf16[128,768]{1,0:T(8,128)(2,1)S(1)} %get-tuple-element.284), channel_id=1, source_target_pairs={{8,0},{10,2},{12,4},{14,6},{16,8},{18,10},{20,12},{22,14},{24,16},... | collective-permute-start | bytes 589832 | tf_op jit(solution)/shard_map/cond/branch_1_fun/ppermute | solution.py:298
  116.5 17.6 %collective-permute-start.51 = (bf16[128,768]{1,0:T(8,128)(2,1)S(1)}, bf16[128,768]{1,0:T(8,128)(2,1)S(1)}, u32[]{:S(2)}, u32[]{:S(2)}) collective-permute-start(bf16[128,768]{1,0:T(8,128)(2,1)S(1)} %get-tuple-element.267), channel_id=1, source_target_pairs={{0,8},{2,10},{4,12},{6,14},{8,16},{10,18},{12,20},{14,22},{16,24},... | collective-permute-start | bytes 589832 | tf_op jit(solution)/shard_map/cond/branch_1_fun/ppermute | solution.py:298
  121.7 14.4 %collective-permute-start.52 = (bf16[128,768]{1,0:T(8,128)(2,1)S(1)}, bf16[128,768]{1,0:T(8,128)(2,1)S(1)}, u32[]{:S(2)}, u32[]{:S(2)}) collective-permute-start(bf16[128,768]{1,0:T(8,128)(2,1)S(1)} %get-tuple-element.268), channel_id=1, source_target_pairs={{8,0},{10,2},{12,4},{14,6},{16,8},{18,10},{20,12},{22,14},{24,16},... | collective-permute-start | bytes 589832 | tf_op jit(solution)/shard_map/cond/branch_1_fun/ppermute | solution.py:298
  123.0 17.6 %collective-permute-start.95 = (bf16[128,768]{1,0:T(8,128)(2,1)S(1)}, bf16[128,768]{1,0:T(8,128)(2,1)S(1)}, u32[]{:S(2)}, u32[]{:S(2)}) collective-permute-start(bf16[128,768]{1,0:T(8,128)(2,1)S(1)} %get-tuple-element.317), channel_id=1, source_target_pairs={{0,8},{2,10},{4,12},{6,14},{8,16},{10,18},{12,20},{14,22},{16,24},... | collective-permute-start | bytes 589832 | tf_op jit(solution)/shard_map/cond/branch_1_fun/ppermute | solution.py:298
  128.2 14.4 %collective-permute-start.96 = (bf16[128,768]{1,0:T(8,128)(2,1)S(1)}, bf16[128,768]{1,0:T(8,128)(2,1)S(1)}, u32[]{:S(2)}, u32[]{:S(2)}) collective-permute-start(bf16[128,768]{1,0:T(8,128)(2,1)S(1)} %get-tuple-element.318), channel_id=1, source_target_pairs={{8,0},{10,2},{12,4},{14,6},{16,8},{18,10},{20,12},{22,14},{24,16},... | collective-permute-start | bytes 589832 | tf_op jit(solution)/shard_map/cond/branch_1_fun/ppermute | solution.py:298
  129.6 17.6 %collective-permute-start.81 = (bf16[128,768]{1,0:T(8,128)(2,1)S(1)}, bf16[128,768]{1,0:T(8,128)(2,1)S(1)}, u32[]{:S(2)}, u32[]{:S(2)}) collective-permute-start(bf16[128,768]{1,0:T(8,128)(2,1)S(1)} %get-tuple-element.301), channel_id=1, source_target_pairs={{0,8},{2,10},{4,12},{6,14},{8,16},{10,18},{12,20},{14,22},{16,24},... | collective-permute-start | bytes 589832 | tf_op jit(solution)/shard_map/cond/branch_1_fun/ppermute | solution.py:298
  134.1 15.0 %collective-permute-start.82 = (bf16[128,768]{1,0:T(8,128)(2,1)S(1)}, bf16[128,768]{1,0:T(8,128)(2,1)S(1)}, u32[]{:S(2)}, u32[]{:S(2)}) collective-permute-start(bf16[128,768]{1,0:T(8,128)(2,1)S(1)} %get-tuple-element.302), channel_id=1, source_target_pairs={{8,0},{10,2},{12,4},{14,6},{16,8},{18,10},{20,12},{22,14},{24,16},... | collective-permute-start | bytes 589832 | tf_op jit(solution)/shard_map/cond/branch_1_fun/ppermute | solution.py:298
  136.1 18.3 %collective-permute-start.67 = (bf16[128,768]{1,0:T(8,128)(2,1)S(1)}, bf16[128,768]{1,0:T(8,128)(2,1)S(1)}, u32[]{:S(2)}, u32[]{:S(2)}) collective-permute-start(bf16[128,768]{1,0:T(8,128)(2,1)S(1)} %get-tuple-element.285), channel_id=1, source_target_pairs={{0,8},{2,10},{4,12},{6,14},{8,16},{10,18},{12,20},{14,22},{16,24},... | collective-permute-start | bytes 589832 | tf_op jit(solution)/shard_map/cond/branch_1_fun/ppermute | solution.py:298
  140.7 15.1 %collective-permute-start.68 = (bf16[128,768]{1,0:T(8,128)(2,1)S(1)}, bf16[128,768]{1,0:T(8,128)(2,1)S(1)}, u32[]{:S(2)}, u32[]{:S(2)}) collective-permute-start(bf16[128,768]{1,0:T(8,128)(2,1)S(1)} %get-tuple-element.286), channel_id=1, source_target_pairs={{8,0},{10,2},{12,4},{14,6},{16,8},{18,10},{20,12},{22,14},{24,16},... | collective-permute-start | bytes 589832 | tf_op jit(solution)/shard_map/cond/branch_1_fun/ppermute | solution.py:298
  142.6 18.3 %collective-permute-start.53 = (bf16[128,768]{1,0:T(8,128)(2,1)S(1)}, bf16[128,768]{1,0:T(8,128)(2,1)S(1)}, u32[]{:S(2)}, u32[]{:S(2)}) collective-permute-start(bf16[128,768]{1,0:T(8,128)(2,1)S(1)} %get-tuple-element.269), channel_id=1, source_target_pairs={{0,8},{2,10},{4,12},{6,14},{8,16},{10,18},{12,20},{14,22},{16,24},... | collective-permute-start | bytes 589832 | tf_op jit(solution)/shard_map/cond/branch_1_fun/ppermute | solution.py:298
  147.2 15.1 %collective-permute-start.54 = (bf16[128,768]{1,0:T(8,128)(2,1)S(1)}, bf16[128,768]{1,0:T(8,128)(2,1)S(1)}, u32[]{:S(2)}, u32[]{:S(2)}) collective-permute-start(bf16[128,768]{1,0:T(8,128)(2,1)S(1)} %get-tuple-element.270), channel_id=1, source_target_pairs={{8,0},{10,2},{12,4},{14,6},{16,8},{18,10},{20,12},{22,14},{24,16},... | collective-permute-start | bytes 589832 | tf_op jit(solution)/shard_map/cond/branch_1_fun/ppermute | solution.py:298
  149.2 17.7 %collective-permute-start.97 = (bf16[128,768]{1,0:T(8,128)(2,1)S(1)}, bf16[128,768]{1,0:T(8,128)(2,1)S(1)}, u32[]{:S(2)}, u32[]{:S(2)}) collective-permute-start(bf16[128,768]{1,0:T(8,128)(2,1)S(1)} %get-tuple-element.319), channel_id=1, source_target_pairs={{0,8},{2,10},{4,12},{6,14},{8,16},{10,18},{12,20},{14,22},{16,24},... | collective-permute-start | bytes 589832 | tf_op jit(solution)/shard_map/cond/branch_1_fun/ppermute | solution.py:298
  154.4 14.4 %collective-permute-start.98 = (bf16[128,768]{1,0:T(8,128)(2,1)S(1)}, bf16[128,768]{1,0:T(8,128)(2,1)S(1)}, u32[]{:S(2)}, u32[]{:S(2)}) collective-permute-start(bf16[128,768]{1,0:T(8,128)(2,1)S(1)} %get-tuple-element.320), channel_id=1, source_target_pairs={{8,0},{10,2},{12,4},{14,6},{16,8},{18,10},{20,12},{22,14},{24,16},... | collective-permute-start | bytes 589832 | tf_op jit(solution)/shard_map/cond/branch_1_fun/ppermute | solution.py:298
  155.7 17.7 %collective-permute-start.83 = (bf16[128,768]{1,0:T(8,128)(2,1)S(1)}, bf16[128,768]{1,0:T(8,128)(2,1)S(1)}, u32[]{:S(2)}, u32[]{:S(2)}) collective-permute-start(bf16[128,768]{1,0:T(8,128)(2,1)S(1)} %get-tuple-element.303), channel_id=1, source_target_pairs={{0,8},{2,10},{4,12},{6,14},{8,16},{10,18},{12,20},{14,22},{16,24},... | collective-permute-start | bytes 589832 | tf_op jit(solution)/shard_map/cond/branch_1_fun/ppermute | solution.py:298
  161.0 14.4 %collective-permute-start.84 = (bf16[128,768]{1,0:T(8,128)(2,1)S(1)}, bf16[128,768]{1,0:T(8,128)(2,1)S(1)}, u32[]{:S(2)}, u32[]{:S(2)}) collective-permute-start(bf16[128,768]{1,0:T(8,128)(2,1)S(1)} %get-tuple-element.304), channel_id=1, source_target_pairs={{8,0},{10,2},{12,4},{14,6},{16,8},{18,10},{20,12},{22,14},{24,16},... | collective-permute-start | bytes 589832 | tf_op jit(solution)/shard_map/cond/branch_1_fun/ppermute | solution.py:298
  162.3 17.7 %collective-permute-start.69 = (bf16[128,768]{1,0:T(8,128)(2,1)S(1)}, bf16[128,768]{1,0:T(8,128)(2,1)S(1)}, u32[]{:S(2)}, u32[]{:S(2)}) collective-permute-start(bf16[128,768]{1,0:T(8,128)(2,1)S(1)} %get-tuple-element.287), channel_id=1, source_target_pairs={{0,8},{2,10},{4,12},{6,14},{8,16},{10,18},{12,20},{14,22},{16,24},... | collective-permute-start | bytes 589832 | tf_op jit(solution)/shard_map/cond/branch_1_fun/ppermute | solution.py:298
  166.9 15.1 %collective-permute-start.70 = (bf16[128,768]{1,0:T(8,128)(2,1)S(1)}, bf16[128,768]{1,0:T(8,128)(2,1)S(1)}, u32[]{:S(2)}, u32[]{:S(2)}) collective-permute-start(bf16[128,768]{1,0:T(8,128)(2,1)S(1)} %get-tuple-element.288), channel_id=1, source_target_pairs={{8,0},{10,2},{12,4},{14,6},{16,8},{18,10},{20,12},{22,14},{24,16},... | collective-permute-start | bytes 589832 | tf_op jit(solution)/shard_map/cond/branch_1_fun/ppermute | solution.py:298
  168.8 18.4 %collective-permute-start.55 = (bf16[128,768]{1,0:T(8,128)(2,1)S(1)}, bf16[128,768]{1,0:T(8,128)(2,1)S(1)}, u32[]{:S(2)}, u32[]{:S(2)}) collective-permute-start(bf16[128,768]{1,0:T(8,128)(2,1)S(1)} %get-tuple-element.271), channel_id=1, source_target_pairs={{0,8},{2,10},{4,12},{6,14},{8,16},{10,18},{12,20},{14,22},{16,24},... | collective-permute-start | bytes 589832 | tf_op jit(solution)/shard_map/cond/branch_1_fun/ppermute | solution.py:298
  173.4 15.1 %collective-permute-start.56 = (bf16[128,768]{1,0:T(8,128)(2,1)S(1)}, bf16[128,768]{1,0:T(8,128)(2,1)S(1)}, u32[]{:S(2)}, u32[]{:S(2)}) collective-permute-start(bf16[128,768]{1,0:T(8,128)(2,1)S(1)} %get-tuple-element.272), channel_id=1, source_target_pairs={{8,0},{10,2},{12,4},{14,6},{16,8},{18,10},{20,12},{22,14},{24,16},... | collective-permute-start | bytes 589832 | tf_op jit(solution)/shard_map/cond/branch_1_fun/ppermute | solution.py:298
  175.4 18.4 %collective-permute-start.99 = (bf16[128,768]{1,0:T(8,128)(2,1)S(1)}, bf16[128,768]{1,0:T(8,128)(2,1)S(1)}, u32[]{:S(2)}, u32[]{:S(2)}) collective-permute-start(bf16[128,768]{1,0:T(8,128)(2,1)S(1)} %get-tuple-element.321), channel_id=1, source_target_pairs={{0,8},{2,10},{4,12},{6,14},{8,16},{10,18},{12,20},{14,22},{16,24},... | collective-permute-start | bytes 589832 | tf_op jit(solution)/shard_map/cond/branch_1_fun/ppermute | solution.py:298
  180.0 15.1 %collective-permute-start.100 = (bf16[128,768]{1,0:T(8,128)(2,1)S(1)}, bf16[128,768]{1,0:T(8,128)(2,1)S(1)}, u32[]{:S(2)}, u32[]{:S(2)}) collective-permute-start(bf16[128,768]{1,0:T(8,128)(2,1)S(1)} %get-tuple-element.322), channel_id=1, source_target_pairs={{8,0},{10,2},{12,4},{14,6},{16,8},{18,10},{20,12},{22,14},{24,16},... | collective-permute-start | bytes 589832 | tf_op jit(solution)/shard_map/cond/branch_1_fun/ppermute | solution.py:298
  182.0 18.7 %collective-permute-start.85 = (bf16[128,768]{1,0:T(8,128)(2,1)S(1)}, bf16[128,768]{1,0:T(8,128)(2,1)S(1)}, u32[]{:S(2)}, u32[]{:S(2)}) collective-permute-start(bf16[128,768]{1,0:T(8,128)(2,1)S(1)} %get-tuple-element.305), channel_id=1, source_target_pairs={{0,8},{2,10},{4,12},{6,14},{8,16},{10,18},{12,20},{14,22},{16,24},... | collective-permute-start | bytes 589832 | tf_op jit(solution)/shard_map/cond/branch_1_fun/ppermute | solution.py:298
  187.2 14.7 %collective-permute-start.86 = (bf16[128,768]{1,0:T(8,128)(2,1)S(1)}, bf16[128,768]{1,0:T(8,128)(2,1)S(1)}, u32[]{:S(2)}, u32[]{:S(2)}) collective-permute-start(bf16[128,768]{1,0:T(8,128)(2,1)S(1)} %get-tuple-element.306), channel_id=1, source_target_pairs={{8,0},{10,2},{12,4},{14,6},{16,8},{18,10},{20,12},{22,14},{24,16},... | collective-permute-start | bytes 589832 | tf_op jit(solution)/shard_map/cond/branch_1_fun/ppermute | solution.py:298
  188.5 14.1 %collective-permute-start.71 = (bf16[128,768]{1,0:T(8,128)(2,1)S(1)}, bf16[128,768]{1,0:T(8,128)(2,1)S(1)}, u32[]{:S(2)}, u32[]{:S(2)}) collective-permute-start(bf16[128,768]{1,0:T(8,128)(2,1)S(1)} %get-tuple-element.289), channel_id=1, source_target_pairs={{0,8},{2,10},{4,12},{6,14},{8,16},{10,18},{12,20},{14,22},{16,24},... | collective-permute-start | bytes 589832 | tf_op jit(solution)/shard_map/cond/branch_1_fun/ppermute | solution.py:298
  193.8 10.8 %collective-permute-start.72 = (bf16[128,768]{1,0:T(8,128)(2,1)S(1)}, bf16[128,768]{1,0:T(8,128)(2,1)S(1)}, u32[]{:S(2)}, u32[]{:S(2)}) collective-permute-start(bf16[128,768]{1,0:T(8,128)(2,1)S(1)} %get-tuple-element.290), channel_id=1, source_target_pairs={{8,0},{10,2},{12,4},{14,6},{16,8},{18,10},{20,12},{22,14},{24,16},... | collective-permute-start | bytes 589832 | tf_op jit(solution)/shard_map/cond/branch_1_fun/ppermute | solution.py:298
  195.1 12.4 %collective-permute-start.57 = (bf16[128,768]{1,0:T(8,128)(2,1)S(1)}, bf16[128,768]{1,0:T(8,128)(2,1)S(1)}, u32[]{:S(2)}, u32[]{:S(2)}) collective-permute-start(bf16[128,768]{1,0:T(8,128)(2,1)S(1)} %get-tuple-element.273), channel_id=1, source_target_pairs={{0,8},{2,10},{4,12},{6,14},{8,16},{10,18},{12,20},{14,22},{16,24},... | collective-permute-start | bytes 589832 | tf_op jit(solution)/shard_map/cond/branch_1_fun/ppermute | solution.py:298
  202.6 11.0 %collective-permute-start.102 = (bf16[128,768]{1,0:T(8,128)(2,1)S(1)}, bf16[128,768]{1,0:T(8,128)(2,1)S(1)}, u32[]{:S(2)}, u32[]{:S(2)}) collective-permute-start(bf16[128,768]{1,0:T(8,128)(2,1)S(1)} %get-tuple-element.325), channel_id=1, source_target_pairs={{0,4},{2,6},{4,0},{6,2},{8,12},{10,14},{12,8},{14,10},{16,20},{18,... | collective-permute-start | bytes 589832 | tf_op jit(solution)/shard_map/cond/branch_1_fun/ppermute | solution.py:294
  204.6 12.3 %collective-permute-start.103 = (bf16[128,768]{1,0:T(8,128)(2,1)S(1)}, bf16[128,768]{1,0:T(8,128)(2,1)S(1)}, u32[]{:S(2)}, u32[]{:S(2)}) collective-permute-start(bf16[128,768]{1,0:T(8,128)(2,1)S(1)} %get-tuple-element.326), channel_id=1, source_target_pairs={{0,6},{2,4},{4,2},{6,0},{8,14},{10,12},{12,10},{14,8},{16,22},{18,... | collective-permute-start | bytes 589832 | tf_op jit(solution)/shard_map/cond/branch_1_fun/ppermute | solution.py:294
  207.5 10.8 %collective-permute-start.87 = (bf16[128,768]{1,0:T(8,128)(2,1)S(1)}, bf16[128,768]{1,0:T(8,128)(2,1)S(1)}, u32[]{:S(2)}, u32[]{:S(2)}) collective-permute-start(bf16[128,768]{1,0:T(8,128)(2,1)S(1)} %get-tuple-element.308), channel_id=1, source_target_pairs={{0,2},{2,0},{4,6},{6,4},{8,10},{10,8},{12,14},{14,12},{16,18},{18,... | collective-permute-start | bytes 589832 | tf_op jit(solution)/shard_map/cond/branch_1_fun/ppermute | solution.py:294
  208.2 11.2 %collective-permute-start.88 = (bf16[128,768]{1,0:T(8,128)(2,1)S(1)}, bf16[128,768]{1,0:T(8,128)(2,1)S(1)}, u32[]{:S(2)}, u32[]{:S(2)}) collective-permute-start(bf16[128,768]{1,0:T(8,128)(2,1)S(1)} %get-tuple-element.309), channel_id=1, source_target_pairs={{0,4},{2,6},{4,0},{6,2},{8,12},{10,14},{12,8},{14,10},{16,20},{18,... | collective-permute-start | bytes 589832 | tf_op jit(solution)/shard_map/cond/branch_1_fun/ppermute | solution.py:294
  209.9 13.0 %collective-permute-start.89 = (bf16[128,768]{1,0:T(8,128)(2,1)S(1)}, bf16[128,768]{1,0:T(8,128)(2,1)S(1)}, u32[]{:S(2)}, u32[]{:S(2)}) collective-permute-start(bf16[128,768]{1,0:T(8,128)(2,1)S(1)} %get-tuple-element.310), channel_id=1, source_target_pairs={{0,6},{2,4},{4,2},{6,0},{8,14},{10,12},{12,10},{14,8},{16,22},{18,... | collective-permute-start | bytes 589832 | tf_op jit(solution)/shard_map/cond/branch_1_fun/ppermute | solution.py:294
  213.6 9.7 %collective-permute-start.73 = (bf16[128,768]{1,0:T(8,128)(2,1)S(1)}, bf16[128,768]{1,0:T(8,128)(2,1)S(1)}, u32[]{:S(2)}, u32[]{:S(2)}) collective-permute-start(bf16[128,768]{1,0:T(8,128)(2,1)S(1)} %get-tuple-element.292), channel_id=1, source_target_pairs={{0,2},{2,0},{4,6},{6,4},{8,10},{10,8},{12,14},{14,12},{16,18},{18,... | collective-permute-start | bytes 589832 | tf_op jit(solution)/shard_map/cond/branch_1_fun/ppermute | solution.py:294
  (28 other events, 221.1 us)
